TPU v7x, 32 devices: a whole 2x2x4 slice. The times are simulated.
32 devices in a mesh: tok: 4 (over z), row: 4 (over y, x), col: 2 (over core).
Axes of the slice: x: 2, y: 2, z: 4, core: 2. Of those that a mesh axis runs over, the one named last changes fastest.
Arguments:
- tokens: bfloat16 [16384, 768], P(('tok', 'row'), 'col'), may hold values from -6 to 6
- cotangent: bfloat16 [16384, 768], P(('tok', 'row'), 'col'), may hold values from -6 to 6
- lengths: int32 [4, 4], P('tok'), may hold values from 1 to 64, 128 in all within a row
- dealing: int32 [512], replicated, may hold values from 0 to 511, as said below
- project_in: bfloat16 [768, 3, 768], P('col', None, 'row'), may hold values from -0.21875 to 0.21875
- project_bias: bfloat16 [2, 768], P(None, 'row'), may hold values from -1.1953125 to 1.1953125
- project_out: bfloat16 [768, 768], P('row', 'col'), may hold values from -4 to 4
- output_bias: bfloat16 [768], P('col'), may hold values from -1.1953125 to 1.1953125
- first_gain: bfloat16 [768], P('col'), may hold values from 0.5 to 1.5
- first_shift: bfloat16 [768], P('col'), may hold values from -1.1953125 to 1.1953125
- up_weight: bfloat16 [768, 3072], P('col', 'row'), may hold values from -0.21875 to 0.21875
- up_bias: bfloat16 [3072], P('row'), may hold values from -1.1953125 to 1.1953125
- down_weight: bfloat16 [3072, 768], P('row', 'col'), may hold values from -0.109375 to 0.109375
- down_bias: bfloat16 [768], P('col'), may hold values from -1.1953125 to 1.1953125
- second_gain: bfloat16 [768], P('col'), may hold values from 0.5 to 1.5
- second_shift: bfloat16 [768], P('col'), may hold values from -1.1953125 to 1.1953125
Outputs:
- output: bfloat16 [16384, 768], P(('tok', 'row'), 'col')
- input_grad: bfloat16 [16384, 768], P(('tok', 'row'), 'col')
- project_in_grad: float32 [768, 3, 768], P('col', None, 'row')
- project_bias_grad: float32 [2, 768], P(None, 'row')
- project_out_grad: float32 [768, 768], P('row', 'col')
- output_bias_grad: float32 [768], P('col')
- first_gain_grad: float32 [768], P('col')
- first_shift_grad: float32 [768], P('col')
- up_weight_grad: float32 [768, 3072], P('col', 'row')
- up_bias_grad: float32 [3072], P('row')
- down_weight_grad: float32 [3072, 768], P('row', 'col')
- down_bias_grad: float32 [768], P('col')
- second_gain_grad: float32 [768], P('col')
- second_shift_grad: float32 [768], P('col')
Inputs may be any that keep to these rules, and one draw needn't show every extreme that they name: lengths[g] are the lengths, counted in blocks of 32 tokens, of group g's 4 sequences in the dealt order; every row sums to 128, and its largest is 64. dealing is a permutation of the blocks. Blocks are numbered in token order, and the blocks in [k * 32, (k + 1) * 32) form shard k, with row index k % 4 and group k // 4. A block keeps its row index: p and dealing[p] lie in shards of one row index. Each shard of the given order has exactly 8 of its blocks dealt into each group.
All inputs are finite; a program needn't handle non-finite values.
Results may differ from a plain program's by a relative error of at most 0.017.
Values may be sent and summed in bfloat16 or wider, within the bound.
No kernel may reach another device: no remote copies, remote signals or barrier semaphores. Data moves between devices by JAX's collectives and lax.ppermute only.
A program may use at most 192 MiB of HBM per device.

v0:
```python
from functools import partial

import jax
import jax.numpy as jnp
from jax import lax
from jax.experimental import pallas as pl
from jax.experimental.pallas import tpu as pltpu
from jax.sharding import PartitionSpec as P

HEAD = 64
LANES = 128
EPSILON = 1e-12
OFF = -1000000000.0
BF = jnp.bfloat16
F32 = jnp.float32
VMEM_LIMIT = 60 * 1024 * 1024


def nn(a, b):
    return lax.dot_general(a, b, (((1,), (0,)), ((), ())), preferred_element_type=F32)


def nt(a, b):
    return lax.dot_general(a, b, (((1,), (1,)), ((), ())), preferred_element_type=F32)


def tn(a, b):
    return lax.dot_general(a, b, (((0,), (0,)), ((), ())), preferred_element_type=F32)


def call(kernel, outs, spaces, scratch=(), out_spaces=None, us=2, blocks=()):
    memory = {"s": pltpu.SMEM, "v": pltpu.VMEM}
    specs = [pl.BlockSpec(memory_space=memory[s]) for s in spaces]
    for operand, (shape, index) in dict(blocks).items():
        specs[operand] = pl.BlockSpec(
            shape, lambda i, index=index, rank=len(shape): (index,) + (0,) * (rank - 1), pipeline_mode=pl.Buffered(1)
        )
    return pl.pallas_call(
        kernel,
        out_shape=[jax.ShapeDtypeStruct(shape, dtype) for shape, dtype in outs],
        grid=(1,) if blocks else (),
        in_specs=specs,
        out_specs=[pl.BlockSpec(memory_space=memory[s]) for s in out_spaces or "v" * len(outs)],
        scratch_shapes=list(scratch),
        compiler_params=pltpu.CompilerParams(vmem_limit_bytes=VMEM_LIMIT),
        cost_estimate=pl.CostEstimate(flops=us * 3 * 10**8, bytes_accessed=us * 10**6, transcendentals=0),
    )


def rows_at(block, size):
    return pl.ds(pl.multiple_of(block * size, size), size)


def send_kernel(sizes, deal, where, x, *outs):
    groups, grid_rows, count, block = sizes
    pieces, table = outs[:groups], outs[groups]
    per_pair = count // groups
    g, r = where[0], where[1]
    mine = g * grid_rows + r
    for d in range(groups):
        base = (lax.rem(g + d, groups) * grid_rows + r) * count

        def step(j, rank):
            source = deal[base + j]
            table[d * per_pair + rank] = lax.rem(source, count)
            return rank + (lax.div(source, count) == mine).astype(jnp.int32)

        lax.fori_loop(0, count, step, jnp.int32(0), unroll=8)
        for rank in range(per_pair):
            rows = rows_at(table[d * per_pair + rank], block)
            pieces[d][rank * block : (rank + 1) * block, :] = x[rows, :]


def send_again_kernel(sizes, table, x, *outs):
    groups, grid_rows, count, block = sizes
    per_pair = count // groups
    for d in range(groups):
        for rank in range(per_pair):
            rows = rows_at(table[d * per_pair + rank], block)
            outs[d][rank * block : (rank + 1) * block, :] = x[rows, :]


def final_kernel(sizes, table, *refs):
    groups, grid_rows, count, block = sizes
    pieces, out = refs[:groups], refs[groups]
    per_pair = count // groups
    for d in range(groups):
        for rank in range(per_pair):
            rows = rows_at(table[(groups - d) % groups * per_pair + rank], block)
            out[rows, :] = pieces[d][rank * block : (rank + 1) * block, :]


def place_kernel(sizes, deal, where, table, tally):
    groups, grid_rows, count, block = sizes
    per_pair = count // groups
    g, r = where[0], where[1]
    for k in range(grid_rows):
        base = (g * grid_rows + (r ^ k)) * count
        for d in range(groups):
            tally[d] = k * count + d * per_pair

        def step(j, carry):
            d = lax.rem(g - lax.div(deal[base + j], grid_rows * count) + groups, groups)
            at = tally[d]
            table[at] = j
            tally[d] = at + 1
            return carry

        lax.fori_loop(0, count, step, jnp.int32(0), unroll=8)


def home_of(j, run, c):
    turn = lax.div(j, run)
    other = (lax.rem(turn, 2) != c).astype(jnp.int32)
    return other * 2 * run + lax.div(turn, 2) * run + lax.rem(j, run)


def arrive_kernel(sizes, run, place, where, *refs):
    groups, grid_rows, count, block = sizes
    pieces, own, other, both = refs[:groups], refs[groups], refs[groups + 1], refs[groups + 2]
    per_pair = count // groups
    for d in range(groups):
        for rank in range(per_pair):
            at = home_of(place[d * per_pair + rank], run, where[2])
            both[rows_at(at, block), :] = pieces[d][rank * block : (rank + 1) * block, :]
    own[...] = both[: own.shape[0], :]
    other[...] = both[own.shape[0] :, :]


def return_kernel(sizes, run, place, where, own, other, *refs):
    groups, grid_rows, count, block = sizes
    outs, both = refs[:groups], refs[groups]
    per_pair = count // groups
    rows = own.shape[0]
    both[:rows, :] = own[...]
    both[rows:, :] = other[other.shape[0] - rows :, :]
    for d in range(groups):
        for rank in range(per_pair):
            at = home_of(place[(groups - d) % groups * per_pair + rank], run, where[2])
            outs[d][rank * block : (rank + 1) * block, :] = both[rows_at(at, block), :]


def sequence_ends(lengths, number):
    ends, total = [], jnp.int32(0)
    for s in range(number):
        total = total + lengths[0, s]
        ends.append(total)
    return ends


def sequence_of(ends, block):
    return sum((block >= end).astype(jnp.int32) for end in ends)


def first_of(ends, block):
    start = jnp.int32(0)
    for end in ends:
        start = jnp.where(block >= end, end, start)
    return start


def last_of(ends, block):
    stop = ends[-1]
    for end in reversed(ends):
        stop = jnp.where(block < end, end, stop)
    return stop


def thirds(v):
    one = v.astype(BF)
    rest = v - one.astype(F32)
    two = rest.astype(BF)
    three = (rest - two.astype(F32)).astype(BF)
    return one.astype(F32), two.astype(F32), three.astype(F32)


def attend_kernel(sizes, layout, heads, seqs, run, place, where, lengths, *refs):
    groups, grid_rows, count, block = sizes
    pieces = refs[: len(layout)]
    weights = refs[len(layout) : len(layout) + 2]
    bias = refs[len(layout) + 2]
    outs = refs[len(layout) + 3 :]
    q_ref, k_ref, v_ref, kt_ref, o_ref, xq_ref, own_ref = outs[:7]
    mixed = outs[7 : 7 + grid_rows]
    x_ref, score_ref, peak_ref, acc_ref = outs[7 + grid_rows :]
    r, c = where[1], where[2]
    ends = sequence_ends(lengths, seqs)
    half = weights[0].shape[1]
    inner = heads * HEAD
    rows = run * block
    for ref, (k, j, start) in zip(pieces, layout):
        for b in range(ref.shape[0] // block):
            at = (r ^ k) * count + place[k * count + start + b]
            x_ref[rows_at(at, block), j * half : (j + 1) * half] = ref[b * block : (b + 1) * block, :]
    local_runs = q_ref.shape[1] // rows
    shard_runs = local_runs // grid_rows
    lane = lax.broadcasted_iota(jnp.int32, (rows, HEAD), 1)
    down = lax.div(lax.broadcasted_iota(jnp.int32, (rows, HEAD), 0), block)
    ones_v = jnp.where(lane < 3, 1.0, 0.0)
    tail_k = (lane >= seqs) & (lane < seqs + 3)
    q_bias, v_bias = bias[0:1, :].astype(F32), bias[1:2, :].astype(F32)

    def project(i, mine):
        at = rows_at(i, rows)
        x0, x1 = x_ref[at, :half], x_ref[at, half:]
        first = 0 if mine else inner
        joined = nt(x0, weights[0][first:, :]) + nt(x1, weights[1][first:, :])
        flipped = nt(weights[0][inner : 2 * inner, :], x0) + nt(weights[1][inner : 2 * inner, :], x1)
        kt_ref[:, at] = flipped.astype(BF)
        seg = sequence_of(ends, down + i * run)
        key_tail = jnp.where((lane == seg) | tail_k, 1.0, 0.0)
        for h in range(heads):
            left = inner - first + h * HEAD
            value = joined[:, left + inner : left + inner + HEAD] + v_bias[:, h * HEAD : (h + 1) * HEAD]
            k_ref[h, at, :] = jnp.concatenate([joined[:, left : left + HEAD], key_tail], axis=1).astype(BF)
            v_ref[h, at, :] = jnp.concatenate([value, ones_v], axis=1).astype(BF)
        return at, joined, seg

    def pair(i, carry):
        project(2 * i + 1 - c, False)
        at, joined, seg = project(2 * i + c, True)
        here = rows_at(i, rows)
        query_tail = jnp.where((lane < seqs) & (lane != seg), OFF, 0.0)
        for h in range(heads):
            query = joined[:, h * HEAD : (h + 1) * HEAD] + q_bias[:, h * HEAD : (h + 1) * HEAD]
            query = query.astype(BF).astype(F32) * (HEAD**-0.5)
            q_ref[h, here, :] = jnp.concatenate([query, query_tail], axis=1).astype(BF)
        xq_ref[here, :] = x_ref[at, :]
        return carry

    lax.fori_loop(0, local_runs, pair, jnp.int32(0))
    own_ref[...] = xq_ref[rows_at(r, rows * shard_runs), :]
    wide = score_ref.shape[3]
    lane_q = lax.broadcasted_iota(jnp.int32, (rows, LANES), 1)

    def one_run(i, carry):
        first = i * 2 * run + c * run
        low = lax.div(first_of(ends, first) * block, wide)
        high = lax.div(last_of(ends, first + run - 1) * block + wide - 1, wide)
        here = rows_at(i, rows)
        peak_ref[...] = jnp.full_like(peak_ref, -3e38)

        def score(j, state):
            for h in range(heads):
                scores = nt(q_ref[h, here, :], k_ref[h, rows_at(j, wide), :])
                score_ref[h, j - low] = scores
                peak = peak_ref[h]
                for t in range(wide // LANES):
                    peak = jnp.maximum(peak, scores[:, t * LANES : (t + 1) * LANES])
                peak_ref[h] = peak
            return state

        lax.fori_loop(low, high, score, jnp.int32(0))
        tops = [jnp.max(peak_ref[h], axis=1, keepdims=True) for h in range(heads)]
        for h in range(heads):
            peak_ref[h] = jnp.broadcast_to(tops[h], (rows, LANES))
        acc_ref[...] = jnp.zeros_like(acc_ref)

        def mix(j, state):
            for h in range(heads):
                peak = jnp.concatenate([peak_ref[h]] * (wide // LANES), axis=1)
                part = jnp.exp(score_ref[h, j - low] - peak).astype(BF)
                acc_ref[h] += nn(part, v_ref[h, rows_at(j, wide), :])
            return state

        lax.fori_loop(low, high, mix, jnp.int32(0))
        for h in range(heads):
            acc = acc_ref[h]
            total = acc[:, HEAD : HEAD + 1]
            o_ref[h, here, :] = (acc[:, :HEAD] / total).astype(BF)
            kept = q_ref[h, here, :].astype(F32)
            for t, term in enumerate(thirds(tops[h] + jnp.log(total))):
                kept = jnp.where(lane_q == HEAD + seqs + t, -term, kept)
            q_ref[h, here, :] = kept.astype(BF)
        return carry

    lax.fori_loop(0, local_runs, one_run, jnp.int32(0))
    for k in range(grid_rows):
        cells = [
            o_ref[h, rows_at((r ^ k) * shard_runs + part, rows), :] for part in range(shard_runs) for h in range(heads)
        ]
        mixed[k][...] = jnp.concatenate(cells, axis=1)


def attend_back_kernel(
    grid_rows, heads_all, start, seqs, run, block, where, lengths, q_ref, k_ref, v_ref, kt_ref, o_ref, *refs
):
    grads = refs[:grid_rows]
    dq_ref, own_ref, other_ref, do_ref, query_acc, key_acc, value_acc = refs[grid_rows:]
    r, c = where[1], where[2]
    heads = q_ref.shape[0]
    ends = sequence_ends(lengths, seqs)
    rows = run * block
    wide = 2 * rows
    local_runs = q_ref.shape[1] // rows
    shard_runs = local_runs // grid_rows
    lane = lax.broadcasted_iota(jnp.int32, (rows, HEAD), 1)
    for k in range(grid_rows):
        for part in range(shard_runs):
            at = rows_at((r ^ k) * shard_runs + part, rows)
            for h in range(heads):
                left = (part * heads_all + start + h) * HEAD
                grad = grads[k][:, left : left + HEAD].astype(F32)
                centre = jnp.sum(grad * o_ref[h, at, :].astype(F32), axis=1, keepdims=True)
                tail = jnp.zeros((rows, HEAD), F32)
                for t, term in enumerate(thirds(centre)):
                    tail = jnp.where(lane == t, -term, tail)
                do_ref[h, at, :] = jnp.concatenate([grad, tail], axis=1).astype(BF)
    key_acc[...] = jnp.zeros_like(key_acc)
    value_acc[...] = jnp.zeros_like(value_acc)

    def one_run(i, carry):
        first = i * 2 * run + c * run
        low = lax.div(first_of(ends, first) * block, wide)
        high = lax.div(last_of(ends, first + run - 1) * block + wide - 1, wide)
        here = rows_at(i, rows)
        query_acc[...] = jnp.zeros_like(query_acc)

        def keys(j, state):
            at = rows_at(j, wide)
            for h in range(heads):
                query, grad = q_ref[h, here, :], do_ref[h, here, :]
                shares = jnp.exp(nt(k_ref[h, at, :], query))
                score_grads = (shares * nt(v_ref[h, at, :], grad)).astype(BF)
                value_acc[h, at, :] += nn(shares.astype(BF), grad)
                key_acc[h, at, :] += nn(score_grads, query)
                query_acc[h] += nn(kt_ref[h * HEAD : (h + 1) * HEAD, at], score_grads)
            return state

        lax.fori_loop(low, high, keys, jnp.int32(0))
        for h in range(heads):
            dq_ref[h, here, :] = (query_acc[h].T * (HEAD**-0.5)).astype(BF)
        return carry

    lax.fori_loop(0, local_runs, one_run, jnp.int32(0))

    def pair(i, carry):
        here = rows_at(i, rows)
        for h in range(heads):
            at = rows_at(2 * i + c, rows)
            own_ref[h, here, :] = jnp.concatenate([key_acc[h, at, :HEAD], value_acc[h, at, :HEAD]], axis=1)
            at = rows_at(2 * i + 1 - c, rows)
            other = jnp.concatenate([key_acc[h, at, :HEAD], value_acc[h, at, :HEAD]], axis=1)
            other_ref[h, here, :] = other.astype(BF)
        return carry

    lax.fori_loop(0, local_runs, pair, jnp.int32(0))


def join_kernel(grid_rows, where, dq_ref, own_ref, got_ref, *refs):
    pieces, joined = refs[:grid_rows], refs[grid_rows]
    r = where[1]
    heads, rows = dq_ref.shape[0], pieces[0].shape[0]
    shard_runs = pieces[0].shape[1] // joined.shape[1]
    for k in range(grid_rows):
        cells = []
        for part in range(shard_runs):
            at = rows_at((r ^ k) * shard_runs + part, rows)
            both = [(own_ref[h, at, :] + got_ref[h, at, :].astype(F32)).astype(BF) for h in range(heads)]
            mine = [dq_ref[h, at, :] for h in range(heads)]
            mine += [b[:, :HEAD] for b in both] + [b[:, HEAD:] for b in both]
            joined[at, :] = jnp.concatenate(mine, axis=1)
            cells += mine
        pieces[k][...] = jnp.concatenate(cells, axis=1)


def project_in_grad_kernel(*refs):
    joined, (xq, own, other) = refs[:-3], refs[-3:]
    half = own.shape[1]
    top, totals = 0, []
    for part in joined:
        wide = part.shape[1]
        own[top : top + wide, :] = tn(part[...], xq[:, :half]).astype(BF)
        other[top : top + wide, :] = tn(part[...], xq[:, half:]).astype(BF)
        totals.append(jnp.sum(part[...].astype(F32), axis=0, keepdims=True))
        top += wide
    total = jnp.concatenate([*totals, jnp.zeros((1, 2 * half - top), F32)], axis=1)
    below = own.shape[0] - top
    sums = jnp.concatenate([total[:, :half], total[:, half:], jnp.zeros((below - 2, half), F32)], axis=0).astype(BF)
    own[top:, :] = sums
    other[top:, :] = sums


def middle_kernel(plan, grid_rows, where, *refs):
    at = 0

    def take(n):
        nonlocal at
        got = refs[at : at + n]
        at += n
        return got

    r, c = where[1], where[2]
    mixed = take(grid_rows)
    (x_ref,) = take(1)
    dy = take(2)
    first = take(2 * grid_rows)
    (gathered,) = take(1)
    second = [gathered.at[(r ^ k) * 2 + (c ^ j)] for k in range(grid_rows) for j in range(2)]
    outs = list(take(1))
    (grad_one_ref,) = take(1)
    mixed_grad = take(grid_rows)
    first_grad, second_grad = take(2), take(2)
    act_ref, up_grad_ref, hidden_ref, down_grad_ref, attn_grad_ref, slope_ref, small = take(7)
    own_rows, half = dy[0].shape
    outs.append(second_grad[1].at[second_grad[1].shape[0] - own_rows :])
    width = 2 * half
    inner = mixed[0].shape[1] // 2
    rows = mixed[0].shape[0]
    part_hidden = first[0].shape[1]
    small[...] = jnp.zeros_like(small)

    def vector(index):
        row = plan["vectors"] + index
        return jnp.concatenate([second[0][row : row + 1, :], second[1][row : row + 1, :]], axis=1).astype(F32)

    output_bias, first_gain, first_shift, down_bias, second_gain, second_shift = (vector(i) for i in range(6))

    def mean(v):
        return jnp.sum(v, axis=1, keepdims=True) / width

    def norm(v):
        centred = v - mean(v)
        inverse = lax.rsqrt(mean(centred * centred) + EPSILON)
        return centred * inverse, inverse

    def norm_back(v, normed, inverse):
        return inverse * (v - mean(v) - normed * mean(v * normed))

    def total(v):
        return jnp.sum(v, axis=0, keepdims=True)

    def keep(row, v):
        small[row : row + 1, : v.shape[1]] += v

    for part in range(2):
        span = slice(part * rows, (part + 1) * rows)
        lanes = slice(part * inner, (part + 1) * inner)
        parts = []
        for j in range(2):
            parts.append(sum(nn(mixed[k][:, lanes], second[2 * k + j][plan["out"], :]) for k in range(grid_rows)))
        attention = jnp.concatenate(parts, axis=1) + output_bias
        normed_one, inverse_one = norm(x_ref[span, :].astype(F32) + attention)
        hidden = normed_one * first_gain + first_shift
        low = hidden.astype(BF)
        hidden_ref[span, :] = low
        downs = [jnp.zeros((rows, half), F32), jnp.zeros((rows, half), F32)]
        for k in range(grid_rows):
            cols = slice(k * part_hidden, (k + 1) * part_hidden)
            upward = nn(low[:, :half], first[2 * k][...]) + nn(low[:, half:], first[2 * k + 1][...])
            bias = [second[2 * k][plan["up_bias"] + u : plan["up_bias"] + u + 1, :] for u in range(part_hidden // half)]
            upward = upward + jnp.concatenate(bias, axis=1).astype(F32)
            bell = (1.0 + lax.erf(upward * (2.0**-0.5))) * 0.5
            slope_ref[:, cols] = bell + upward * jnp.exp(upward * upward * -0.5) * 0.3989422804014327
            act = (upward * bell).astype(BF)
            act_ref[span, cols] = act
            for j in range(2):
                downs[j] = downs[j] + nn(act, second[2 * k + j][plan["down"], :])
        downward = jnp.concatenate(downs, axis=1) + down_bias
        normed_two, inverse_two = norm(hidden + downward)
        final = (normed_two * second_gain + second_shift).astype(BF)
        outs[0][span, :] = final[:, :half]
        outs[1][span, :] = final[:, half:]
        grad_out = jnp.concatenate([dy[0][span, :], dy[1][span, :]], axis=1).astype(F32)
        keep(0, total(grad_out * normed_two))
        keep(1, total(grad_out))
        grad_two = norm_back(grad_out * second_gain, normed_two, inverse_two)
        down_grad = grad_two.astype(BF)
        down_grad_ref[span, :] = down_grad
        keep(4, total(down_grad.astype(F32)))
        grads = [grad_two[:, :half], grad_two[:, half:]]
        for k in range(grid_rows):
            cols = slice(k * part_hidden, (k + 1) * part_hidden)
            act_grad = nt(down_grad[:, :half], second[2 * k][plan["down"], :]) + nt(
                down_grad[:, half:], second[2 * k + 1][plan["down"], :]
            )
            up_grad = (act_grad * slope_ref[:, cols]).astype(BF)
            up_grad_ref[span, cols] = up_grad
            keep(8 + k, total(up_grad.astype(F32)))
            for j in range(2):
                grads[j] = grads[j] + nt(up_grad, first[2 * k + j][...])
        grad_hidden = jnp.concatenate(grads, axis=1)
        keep(2, total(grad_hidden * normed_one))
        keep(3, total(grad_hidden))
        grad_one = norm_back(grad_hidden * first_gain, normed_one, inverse_one)
        grad_one_ref[span, :] = grad_one
        attn_grad = grad_one.astype(BF)
        attn_grad_ref[span, :] = attn_grad
        keep(5, total(attn_grad.astype(F32)))
        for k in range(grid_rows):
            back = nt(attn_grad[:, :half], second[2 * k][plan["out"], :]) + nt(
                attn_grad[:, half:], second[2 * k + 1][plan["out"], :]
            )
            mixed_grad[k][:, lanes] = back.astype(BF)

    for j in range(2):
        side = slice(j * half, (j + 1) * half)
        for place, k in enumerate(plan["second_order"]):
            cols = slice(k * part_hidden, (k + 1) * part_hidden)
            grad = second_grad[j].at[place * plan["rows"] : (place + 1) * plan["rows"]]
            grad[plan["down"], :] = tn(act_ref[:, cols], down_grad_ref[:, side]).astype(BF)
            back = tn(mixed[k][:, :inner], attn_grad_ref[:rows, side])
            back = back + tn(mixed[k][:, inner:], attn_grad_ref[rows:, side])
            grad[plan["out"], :] = back.astype(BF)
            sums = [small[:6, side]] + [small[8 + k : 9 + k, u * half : (u + 1) * half] for u in range(part_hidden // half)]
            sums += [jnp.zeros((32 - 6 - part_hidden // half, half), F32)]
            grad[plan["sums"], :] = jnp.concatenate(sums, axis=0).astype(BF)
        for place, k in enumerate(plan["first_order"]):
            cols = slice(k * part_hidden, (k + 1) * part_hidden)
            first_grad[j][place, :, :] = tn(hidden_ref[:, side], up_grad_ref[:, cols]).astype(BF)


def input_grad_kernel(grid_rows, parts, where, *refs):
    pieces = [refs[i * grid_rows : (i + 1) * grid_rows] for i in range(parts)]
    weight, grad_one, own, other = refs[parts * grid_rows :]
    r, c = where[1], where[2]
    half = own.shape[1]
    rows = pieces[0][0].shape[0]
    for run in range(2):
        span = slice(run * rows, (run + 1) * rows)
        for j, out in enumerate((own, other)):
            total = grad_one[span, j * half : (j + 1) * half]
            for k in range(grid_rows):
                top = 0
                for part in pieces:
                    wide = part[k].shape[1] // 2
                    held = weight[(r ^ k) * 2 + (c ^ j), top : top + wide, :]
                    total = total + nn(part[k][:, run * wide : (run + 1) * wide], held)
                    top += wide
            out[span, :] = total.astype(BF)


def shift(array, axis, to):
    return lax.ppermute(array, axis, [(i, to(i)) for i in range(lax.axis_size(axis))])


def to_row(array, k):
    return shift(array, "row", lambda i: i ^ k)


def to_col(array):
    return shift(array, "col", lambda i: 1 - i)


def after(array, *earlier):
    return lax.optimization_barrier((array, *earlier))[0]


def gather_near(array):
    return to_row(array, 1), to_row(array, 2)


def gather_row(array, near, side, cut):
    got = [(0, 0, array), (1, 0, near), (2, 0, side), (3, 0, to_row(near[:cut], 2))]
    return got + ([(3, cut, to_row(side[cut:], 1))] if cut < array.shape[0] else [])


def after_all(arrays, *earlier):
    return lax.optimization_barrier((*arrays, *earlier))[: len(arrays)]


def add(*arrays):
    return sum(a.astype(F32) for a in arrays).astype(BF)


def reduce_first(own, got):
    return add(own[2:], got[2:])


def reduce_groups(array, group):
    if lax.axis_size("tok") != 4:
        return lax.psum(array, "tok")
    side = (group ^ (group >> 1)) & 1
    middle = array.shape[0] // 2
    low, high = array[:middle], array[middle:]
    half = add(jnp.where(side == 0, low, high), shift(jnp.where(side == 0, high, low), "tok", lambda i: i ^ 1))
    half = add(half, shift(half, "tok", lambda i: i ^ 3))
    rest = shift(half, "tok", lambda i: i ^ 1)
    return jnp.concatenate([jnp.where(side == 0, half, rest), jnp.where(side == 0, rest, half)], axis=0)


def local(
    tokens,
    cotangent,
    lengths,
    dealing,
    project_in,
    project_bias,
    project_out,
    output_bias,
    first_gain,
    first_shift,
    up_weight,
    up_bias,
    down_weight,
    down_bias,
    second_gain,
    second_shift,
):
    groups, grid_rows = lax.axis_size("tok"), lax.axis_size("row")
    group, row, col = lax.axis_index("tok"), lax.axis_index("row"), lax.axis_index("col")
    where = jnp.stack([group, row, col]).astype(jnp.int32)
    shard_rows, half = tokens.shape
    width = 2 * half
    count = dealing.shape[0] // (groups * grid_rows)
    block = shard_rows // count
    sizes = (groups, grid_rows, count, block)
    seqs = lengths.shape[1]
    inner = project_bias.shape[1]
    heads = inner // HEAD
    hidden_part = up_weight.shape[1]
    run = count // 4
    rows = run * block
    own_rows = shard_rows // 2
    half_rows = own_rows * grid_rows
    wide = 3 * inner
    per_pair = count // groups
    piece = (per_pair * block, half)
    shard = (shard_rows, half)
    both = pltpu.VMEM(shard, BF)

    def exchange(pieces):
        return [shift(p, "tok", lambda i, d=d: (i + d) % groups) if d else p for d, p in enumerate(pieces)]

    joined_weight = project_in.transpose(1, 2, 0).reshape(wide, half)
    out_rows = slice(hidden_part, hidden_part + inner)
    plan = {
        "down": slice(0, hidden_part),
        "out": out_rows,
        "vectors": out_rows.stop,
        "up_bias": out_rows.stop + 6,
        "sums": slice(out_rows.stop, out_rows.stop + 32),
        "rows": out_rows.stop + 32,
        "first_order": (0, 2, 1, 3),
        "second_order": (0, 1, 2, 3),
    }

    *sent, table = call(
        partial(send_kernel, sizes), [(piece, BF)] * groups + [((count + 8,), jnp.int32)], "ssv",
        out_spaces="v" * groups + "s",
    )(dealing, where, tokens)
    (place,) = call(partial(place_kernel, sizes), [((grid_rows * count,), jnp.int32)], "ss", [pltpu.SMEM((groups,), jnp.int32)], "s", 2)(
        dealing, where
    )
    got = exchange(sent)
    vectors = [output_bias, first_gain, first_shift, down_bias, second_gain, second_shift, up_bias]
    vectors = after(jnp.concatenate(vectors), *got).reshape(8, half)
    second_weights = jnp.concatenate(
        [after(down_weight, *got), after(project_out, *got), jnp.pad(vectors, ((0, 8), (0, 0)))], axis=0
    )
    first_near = gather_near(up_weight)
    chunk = jnp.concatenate(after_all(got, place, *first_near), axis=0)
    chunk_near = gather_near(chunk)
    dy_sent = call(partial(send_again_kernel, sizes), [(piece, BF)] * groups, "sv")(table, after(cotangent, *got))
    chunk_near = after_all(chunk_near, *dy_sent)
    layout, pieces = [], []
    parts = gather_row(chunk, *chunk_near, shard_rows // 2)
    for k, top, part in parts:
        layout += [(k, 0, top // block), (k, 1, top // block)]
        pieces += [part, to_col(part)]
    far = [part for k, _, part in parts if k == 3]
    second_all = lax.all_gather(after(second_weights, *chunk_near), ("row", "col"))
    first_row = after_all((up_weight, *first_near), *chunk_near)
    first_all = [part for weight in first_row for part in (weight, to_col(weight))]
    pieces[0] = after(pieces[0], *first_all)
    first_far = to_row(after(up_weight, *far), 3)
    dy_got = exchange(after_all(dy_sent, *far))
    wide_keys = 2 * rows
    q, k, v, kt, mixed_own, xq, x_own, *mixed = call(
        partial(attend_kernel, sizes, layout, heads, seqs, run),
        [
            ((heads, half_rows, LANES), BF),
            ((heads, 2 * half_rows, LANES), BF),
            ((heads, 2 * half_rows, LANES), BF),
            ((inner, 2 * half_rows), BF),
            ((heads, half_rows, HEAD), BF),
            ((half_rows, width), BF),
            ((own_rows, width), BF),
        ]
        + [((rows, 2 * inner), BF)] * grid_rows,
        "sss" + "v" * (len(pieces) + 3),
        [
            pltpu.VMEM((2 * half_rows, width), BF),
            pltpu.VMEM((heads, 2 * half_rows // wide_keys, rows, wide_keys), F32),
            pltpu.VMEM((heads, rows, LANES), F32),
            pltpu.VMEM((heads, rows, LANES), F32),
        ],
        us=47,
    )(place, where, lengths, *pieces, joined_weight, to_col(joined_weight), project_bias)

    mixed = after_all(mixed, *dy_got, first_far)
    first_far = after(first_far, mixed[0])
    first_all += [first_far, to_col(first_far)]
    dy_own, dy_other = call(
        partial(arrive_kernel, sizes, run), [((own_rows, half), BF)] * 2, "ss" + "v" * groups, [both]
    )(place, where, *dy_got)
    dy = [dy_own, to_col(dy_other)]

    def leave(own, other):
        return call(partial(return_kernel, sizes, run), [(piece, BF)] * groups, "ssvv", [both])(place, where, own, other)

    def come_back(pieces):
        return call(partial(final_kernel, sizes), [(shard, BF)], "s" + "v" * groups)(table, *pieces)[0]

    mixed_got = [to_row(m, i) if i else m for i, m in enumerate(mixed)]
    parts = ((0, heads - 1), (heads - 1, 1))
    held = [(i * heads + start) * HEAD for start, _ in parts for i in range(3)]
    spans = [number * HEAD for _, number in parts for _ in range(3)]
    split = jnp.concatenate([joined_weight[top : top + span] for top, span in zip(held, spans)], axis=0)
    joined_all = lax.all_gather(after(split, mixed[0]), ("row", "col"))
    hidden_all = grid_rows * hidden_part
    second_rows = plan["rows"]
    out0, grad_one, *rest = call(
        partial(middle_kernel, plan, grid_rows),
        [((own_rows, half), BF), ((own_rows, width), F32)]
        + [((rows, 2 * inner), BF)] * grid_rows
        + [((grid_rows, half, hidden_part), BF)] * 2
        + [((grid_rows * second_rows, half), BF), ((grid_rows * second_rows + own_rows, half), BF)],
        "s" + "v" * (grid_rows + 3 + 2 * grid_rows + 1),
        [
            pltpu.VMEM((own_rows, hidden_all), BF),
            pltpu.VMEM((own_rows, hidden_all), BF),
            pltpu.VMEM((own_rows, width), BF),
            pltpu.VMEM((own_rows, width), BF),
            pltpu.VMEM((own_rows, width), BF),
            pltpu.VMEM((rows, hidden_all), F32),
            pltpu.VMEM((16, width), F32),
        ],
        us=42,
    )(where, *mixed_got, x_own, *dy, *first_all, second_all)
    mixed_grad = rest[:grid_rows]
    first_own, first_other, second_own, second_other = rest[grid_rows:]
    mixed_grad_got = [to_row(m, i) if i else m for i, m in enumerate(mixed_grad)]
    first_got, second_got = to_col(first_other), to_col(second_other)
    out_pieces = leave(out0, second_got)
    first_leaving = add(first_own[2:], first_got[2:])
    second_cut = [slice(i * second_rows, (i + 1) * second_rows) for i in range(grid_rows)]
    second_far = slice(2 * second_rows, 4 * second_rows)
    second_leaving = add(second_own[second_far], second_got[second_far])
    first_leaving, second_leaving, *out_pieces = after_all((first_leaving, second_leaving, *out_pieces), *mixed_grad_got)
    first_came, second_came = to_row(first_leaving, 1), to_row(second_leaving, 2)
    out_got = exchange(out_pieces)
    mixed_grad_got[0] = after(mixed_grad_got[0], first_leaving, second_leaving, *out_pieces)

    def back(start, number, grads):
        held = {
            2: ((number, half_rows, LANES), start // number),
            3: ((number, 2 * half_rows, LANES), start // number),
            4: ((number, 2 * half_rows, LANES), start // number),
            5: ((number * HEAD, 2 * half_rows), start // number),
            6: ((number, half_rows, HEAD), start // number),
        }
        return call(
            partial(attend_back_kernel, grid_rows, heads, start, seqs, run, block),
            [
                ((number, half_rows, HEAD), BF),
                ((number, half_rows, LANES), F32),
                ((number, half_rows, LANES), BF),
            ],
            "ss" + "v" * (5 + grid_rows),
            [
                pltpu.VMEM((number, half_rows, LANES), BF),
                pltpu.VMEM((number, HEAD, rows), F32),
                pltpu.VMEM((number, 2 * half_rows, LANES), F32),
                pltpu.VMEM((number, 2 * half_rows, LANES), F32),
            ],
            us=16 * number,
            blocks=held,
        )(where, lengths, q, k, v, kt, mixed_own, *grads)

    def join(dq, own, got):
        number = dq.shape[0]
        *pieces, joined = call(
            partial(join_kernel, grid_rows),
            [((rows, 2 * number * 3 * HEAD), BF)] * grid_rows + [((half_rows, number * 3 * HEAD), BF)],
            "svvv",
            us=2 * number,
        )(where, dq, own, got)
        return [to_row(m, i) if i else m for i, m in enumerate(pieces)], pieces, joined

    dq, kv_own, kv_other = back(0, heads - 1, mixed_grad_got)
    kv_other = after(kv_other, first_came, second_came, *out_got)
    kv_got = to_col(kv_other)
    first_own, second_own, out_got[0] = after_all((first_own, second_own, out_got[0]), dq)
    first_parting = add(first_own[1], first_got[1], first_came[1])
    second_parting = add(second_own[second_cut[1]], second_got[second_cut[1]], second_came[second_rows:])
    first_last, second_last = to_row(first_parting, 2), to_row(second_parting, 1)
    joined_got, leaving, joined = join(dq, kv_own, kv_got)
    mixed_grad_got[0] = after(mixed_grad_got[0], first_parting, second_parting, *leaving)
    dq, kv_own, kv_other = back(heads - 1, 1, mixed_grad_got)
    kv_other = after(kv_other, first_last, second_last, *joined_got)
    first_own, second_own, out_got[0] = after_all((first_own, second_own, out_got[0]), dq)
    first_sum = add(first_own[0], first_got[0], first_came[0], first_last)
    second_sum = add(second_own[second_cut[0]], second_got[second_cut[0]], second_came[:second_rows], second_last)
    kv_got = after(to_col(kv_other), first_sum, second_sum)
    last_got, leaving, last_joined = join(dq, kv_own, kv_got)
    first_sum, second_sum = reduce_groups(first_sum, group), reduce_groups(second_sum, group)
    output = come_back(out_got)
    dx_own, dx_other = call(
        partial(input_grad_kernel, grid_rows, 2), [((own_rows, half), BF)] * 2, "s" + "v" * (2 * grid_rows + 2), us=7
    )(where, *joined_got, *last_got, joined_all, grad_one)
    dx_pieces = leave(dx_own, to_col(dx_other))
    in_own, in_other = call(project_in_grad_kernel, [((wide + 32, half), BF)] * 2, "vvv", us=6)(
        joined, after(last_joined, *dx_pieces), xq
    )
    in_sum = reduce_groups(add(in_own, to_col(in_other)), group)
    dx_got = exchange(dx_pieces)
    input_grad = come_back(dx_got)

    tops = [sum(spans[:i]) for i in range(6)]
    in_parts = [in_sum[top : top + span] for top, span in zip(tops, spans)]
    in_parts = [jnp.concatenate([in_parts[i], in_parts[3 + i]], axis=0) for i in range(3)]
    project_in_grad = jnp.stack(in_parts).transpose(2, 0, 1)
    sums = in_sum[wide : wide + 2].reshape(2 * half)
    in_sums = [sums[top : top + span] for top, span in zip(tops, spans)]
    sums = [jnp.concatenate([in_sums[i], in_sums[3 + i]]) for i in (0, 2)]
    tail = second_sum[plan["sums"]].astype(F32)
    return (
        output,
        input_grad,
        project_in_grad.astype(F32),
        jnp.stack(sums).astype(F32),
        second_sum[out_rows].astype(F32),
        tail[5],
        tail[2],
        tail[3],
        first_sum.astype(F32),
        tail[6:8].reshape(hidden_part),
        second_sum[:hidden_part].astype(F32),
        tail[4],
        tail[0],
        tail[1],
    )


def solution(mesh):
    stream, grid = P(("tok", "row"), "col"), P("row", "col")
    joined, mids, cols = P("col", None, "row"), P("col", "row"), P("col")
    in_specs = (
        stream, stream, P("tok", None), P(), joined, P(None, "row"), grid, cols,
        cols, cols, mids, P("row"), grid, cols, cols, cols,
    )
    out_specs = (
        stream, stream, joined, P(None, "row"), grid, cols,
        cols, cols, mids, P("row"), grid, cols, cols, cols,
    )
    return jax.shard_map(local, mesh=mesh, in_specs=in_specs, out_specs=out_specs, check_vma=False)
```

profile of v0, /device:TPU:0, one launch (start us, length us, event | category | flops | bytes accessed | tf_op | source)
XLA Modules:
  0.0 389.6 jit_solution(14408871529662809322)
XLA Ops:
  25.2 6.7 %collective-permute-done.1 = bf16[256,384]{1,0:T(8,128)(2,1)S(1)} collective-permute-done((bf16[256,384]{1,0:T(8,128)(2,1)}, bf16[256,384]{1,0:T(8,128)(2,1)S(1)}, u32[]{:S(2)}, u32[]{:S(2)}) %collective-permute-start.1) | collective-permute-done | bytes 196640 | tf_op jit(solution)/shard_map/ppermute | solution.py:534
  37.8 13.7 %collective-permute-done.5.refs_2_ = bf16[1024,384]{1,0:T(8,128)(2,1)S(1)} collective-permute-done((bf16[1024,384]{1,0:T(8,128)(2,1)S(1)}, bf16[1024,384]{1,0:T(8,128)(2,1)S(1)}, u32[]{:S(2)}, u32[]{:S(2)}) %collective-permute-start.5) | collective-permute-done | bytes 786464 | tf_op jit(solution)/shard_map/ppermute | solution.py:534
  55.2 8.5 %collective-permute-done.13.refs_6_ = bf16[512,384]{1,0:T(8,128)(2,1)S(1)} collective-permute-done((bf16[512,384]{1,0:T(8,128)(2,1)S(1)}, bf16[512,384]{1,0:T(8,128)(2,1)S(1)}, u32[]{:S(2)}, u32[]{:S(2)}) %collective-permute-start.13) | collective-permute-done | bytes 393248 | tf_op jit(solution)/shard_map/ppermute | solution.py:534
  66.6 7.9 %collective-permute-start.18 = (bf16[256,384]{1,0:T(8,128)(2,1)}, bf16[256,384]{1,0:T(8,128)(2,1)S(1)}, u32[]{:S(2)}, u32[]{:S(2)}) collective-permute-start(bf16[256,384]{1,0:T(8,128)(2,1)} %get-tuple-element.143), channel_id=1, source_target_pairs={{0,8},{8,16},{16,24},{24,0},{1,9},{9,17},{17,25},{25,1},{2,10},{10... | collective-permute-start | bytes 589832 | tf_op jit(solution)/shard_map/ppermute | solution.py:534
  74.4 5.0 %collective-permute-start.20 = (bf16[256,384]{1,0:T(8,128)(2,1)}, bf16[256,384]{1,0:T(8,128)(2,1)}, u32[]{:S(2)}, u32[]{:S(2)}) collective-permute-start(bf16[256,384]{1,0:T(8,128)(2,1)} %get-tuple-element.145), channel_id=1, source_target_pairs={{0,24},{8,0},{16,8},{24,16},{1,25},{9,1},{17,9},{25,17},{2,26},{10... | collective-permute-start | bytes 589832 | tf_op jit(solution)/shard_map/ppermute | solution.py:534
  80.3 3.4 collective-permute-start.21
  83.8 46.6 %shard_map.266 = (bf16[3,2048,128]{2,1,0:T(8,128)(2,1)}, bf16[3,4096,128]{2,1,0:T(8,128)(2,1)}, bf16[3,4096,128]{2,1,0:T(8,128)(2,1)}, bf16[192,4096]{1,0:T(8,12...) custom-call(s32[128]{0:T(128)} %shard_map.264.place, ...), custom_call_target="tpu_custom_call" | custom-call | flops 14099999744 | bytes 47000000 | tf_op jit(solution)/shard_map/pallas_call | solution.py:669
  137.2 4.2 %collective-permute-done.22.refs_1_ = bf16[256,384]{1,0:T(8,128)(2,1)S(1)} collective-permute-done((bf16[256,384]{1,0:T(8,128)(2,1)S(1)}, bf16[256,384]{1,0:T(8,128)(2,1)S(1)}, u32[]{:S(2)}, u32[]{:S(2)}) %collective-permute-start.22) | collective-permute-done | bytes 196640 | tf_op jit(solution)/shard_map/ppermute | solution.py:534
  141.4 3.8 collective-permute-done.23.refs_2_
  146.2 36.2 %shard_map.268 = (bf16[512,384]{1,0:T(8,128)(2,1)}, f32[512,768]{1,0:T(8,128)}, bf16[256,384]{1,0:T(8,128)(2,1)}, bf16[256,384]{1,0:T(8,128)(2,1)}, bf16[256,384...) custom-call(s32[3]{0:T(128)} %pad_add_fusion.where, ...), custom_call_target="tpu_custom_call" | custom-call | flops 12600000512 | bytes 42000000 | tf_op jit(solution)/shard_map/pallas_call | solution.py:713
  206.2 3.8 collective-permute-start.36
  210.0 37.1 %shard_map.270 = (bf16[2,2048,64]{2,1,0:T(8,128)(2,1)}, f32[2,2048,128]{2,1,0:T(8,128)}, bf16[2,2048,128]{2,1,0:T(8,128)(2,1)}) custom-call(s32[3]{0:T(128)} %pad_add_fusion.where, s32[1,4]{1,0:T(1,128)} %lengths.5, bf16[3,2048,128]{2,1,0:T(8,128)(2,1)} %get-tuple-element.173.q_ref, bf16[3,4096,128]{2,1,0:T(8,128)(2,1)} %get-tuple-element.174.k_ref, ...), custom_call_target="tpu_custom_call" | custom-call | flops 9600000000 | bytes 32000000 | tf_op jit(solution)/shard_map/pallas_call | solution.py:753
  252.2 4.3 %shard_map.271 = (bf16[256,768]{1,0:T(8,128)(2,1)}, bf16[256,768]{1,0:T(8,128)(2,1)}, bf16[256,768]{1,0:T(8,128)(2,1)}, bf16[256,768]{1,0:T(8,128)(2,1)}, bf16[2048,384]{1,0:T(8,128)(2,1)}) custom-call(s32[3]{0:T(128)} %pad_add_fusion.where, bf16[2,2048,64]{2,1,0:T(8,128)(2,1)} %get-tuple-element.184.dq_ref, f32[2,2048,128]{2,1,0:T(8,128)} %get-tuple-element.188.own_ref, ...), custom_call_target="tpu_custom_call" | custom-call | flops 1200000000 | bytes 4000000 | tf_op jit(solution)/shard_map/pallas_call | solution.py:773
  260.0 22.1 %shard_map.272 = (bf16[1,2048,64]{2,1,0:T(8,128)(2,1)}, f32[1,2048,128]{2,1,0:T(8,128)}, bf16[1,2048,128]{2,1,0:T(8,128)(2,1)}) custom-call(s32[3]{0:T(128)} %pad_add_fusion.where, s32[1,4]{1,0:T(1,128)} %lengths.5, bf16[3,2048,128]{2,1,0:T(8,128)(2,1)} %get-tuple-element.173.q_ref, bf16[3,4096,128]{2,1,0:T(8,128)(2,1)} %get-tuple-element.174.k_ref, ...), custom_call_target="tpu_custom_call" | custom-call | flops 4800000000 | bytes 16000000 | tf_op jit(solution)/shard_map/pallas_call | solution.py:753
  284.0 4.9 %collective-permute-done.40.refs_3_ = bf16[256,768]{1,0:T(8,128)(2,1)} collective-permute-done((bf16[256,768]{1,0:T(8,128)(2,1)}, bf16[256,768]{1,0:T(8,128)(2,1)}, u32[]{:S(2)}, u32[]{:S(2)}) %collective-permute-start.40) | collective-permute-done | bytes 393248 | tf_op jit(solution)/shard_map/ppermute | solution.py:534
  299.8 4.2 %collective-permute-done.44.refs_5_ = bf16[256,384]{1,0:T(8,128)(2,1)S(1)} collective-permute-done((bf16[256,384]{1,0:T(8,128)(2,1)}, bf16[256,384]{1,0:T(8,128)(2,1)S(1)}, u32[]{:S(2)}, u32[]{:S(2)}) %collective-permute-start.44) | collective-permute-done | bytes 196640 | tf_op jit(solution)/shard_map/ppermute | solution.py:534
  304.0 3.9 %collective-permute-done.45.refs_6_ = bf16[256,384]{1,0:T(8,128)(2,1)} collective-permute-done((bf16[256,384]{1,0:T(8,128)(2,1)}, bf16[256,384]{1,0:T(8,128)(2,1)}, u32[]{:S(2)}, u32[]{:S(2)}) %collective-permute-start.45) | collective-permute-done | bytes 196640 | tf_op jit(solution)/shard_map/ppermute | solution.py:534
  308.0 7.1 %shard_map.275 = (bf16[512,384]{1,0:T(8,128)(2,1)}, bf16[512,384]{1,0:T(8,128)(2,1)}) custom-call(s32[3]{0:T(128)} %pad_add_fusion.where, bf16[256,768]{1,0:T(8,128)(2,1)} %get-tuple-element.191.refs_0_, bf16[256,768]{1,0:T(8,128)(2,1)} %collective-permute-done.38.refs_1_, bf16[256,768]{1,0:T(8,128)(2,1)} %collective-permute-done.39.refs_2_, ...), custom_call_target="tpu_custom_call" | custom-call | flops 2100000000 | bytes 7000000 | tf_op jit(solution)/shard_map/pallas_call | solution.py:799
  320.2 6.5 %shard_map.278 = (bf16[608,384]{1,0:T(8,128)(2,1)}, bf16[608,384]{1,0:T(8,128)(2,1)}) custom-call(bf16[2048,384]{1,0:T(8,128)(2,1)} %get-tuple-element.216.refs_0_, bf16[2048,192]{1,0:T(8,128)(2,1)} %get-tuple-element.218.refs_1_, bf16[2048,768]{1,0:T(8,128)(2,1)} %get-tuple-element.219.refs_2_), custom_call_target="tpu_custom_call" | custom-call | flops 1800000000 | bytes 6000000 | tf_op jit(solution)/shard_map/pallas_call | solution.py:803
  328.9 7.7 %collective-permute-start.57 = (bf16[496,384]{1,0:T(8,128)(2,1)S(1)}, bf16[496,384]{1,0:T(8,128)(2,1)S(1)}, u32[]{:S(2)}, u32[]{:S(2)}) collective-permute-start(bf16[496,384]{1,0:T(8,128)(2,1)S(1)} %add_convert_fusion.6), channel_id=1, source_target_pairs={{0,8},{8,0},{16,24},{24,16},{1,9},{9,1},{17,25},{25,17},{2,10},{10... | collective-permute-start | bytes 1142792 | tf_op jit(solution)/shard_map/ppermute | solution.py:534
  338.1 8.2 %collective-permute-done.57 = bf16[496,384]{1,0:T(8,128)(2,1)S(1)} collective-permute-done((bf16[496,384]{1,0:T(8,128)(2,1)S(1)}, bf16[496,384]{1,0:T(8,128)(2,1)S(1)}, u32[]{:S(2)}, u32[]{:S(2)}) %collective-permute-start.57) | collective-permute-done | bytes 380960 | tf_op jit(solution)/shard_map/ppermute | solution.py:534
  346.4 3.9 %collective-permute-done.52 = bf16[304,384]{1,0:T(8,128)(2,1)S(1)} collective-permute-done((bf16[304,384]{1,0:T(8,128)(2,1)S(1)}, bf16[304,384]{1,0:T(8,128)(2,1)S(1)}, u32[]{:S(2)}, u32[]{:S(2)}) %collective-permute-start.52) | collective-permute-done | bytes 233504 | tf_op jit(solution)/shard_map/ppermute | solution.py:534
  357.4 3.7 collective-permute-done.53
  361.2 12.2 %collective-permute-start.54 = (bf16[304,384]{1,0:T(8,128)(2,1)S(1)}, bf16[304,384]{1,0:T(8,128)(2,1)S(1)}, u32[]{:S(2)}, u32[]{:S(2)}) collective-permute-start(bf16[304,384]{1,0:T(8,128)(2,1)S(1)} %add_convert_fusion.10), channel_id=1, source_target_pairs={{0,8},{8,0},{16,24},{24,16},{1,9},{9,1},{17,25},{25,17},{2,10},{10... | collective-permute-start | bytes 700424 | tf_op jit(solution)/shard_map/ppermute | solution.py:534
  (286 shorter events, 108.4 us)
Async XLA Ops:
  7.2 138.1 %all-gather.5.cloned.1.call-start = ((), (), s32[]{:S(2)}) async-start(), calls=%async_computation | async-start | bytes 6746112 | tf_op jit(solution)/shard_map/all_gather | solution.py:662
  7.2 24.7 %collective-permute-start.3 = (bf16[384,768]{1,0:T(8,128)(2,1)}, bf16[384,768]{1,0:T(8,128)(2,1)}, u32[]{:S(2)}, u32[]{:S(2)}) collective-permute-start(bf16[384,768]{1,0:T(8,128)(2,1)} %refs_7_), channel_id=1, source_target_pairs={{0,2},{2,0},{4,6},{6,4},{1,3},{3,1},{5,7},{7,5},{8,10},{10,8},{12,... | collective-permute-start | bytes 1769480 | tf_op jit(solution)/shard_map/ppermute | solution.py:534
  10.2 21.7 %collective-permute-start.4 = (bf16[384,768]{1,0:T(8,128)(2,1)}, bf16[384,768]{1,0:T(8,128)(2,1)}, u32[]{:S(2)}, u32[]{:S(2)}) collective-permute-start(bf16[384,768]{1,0:T(8,128)(2,1)} %refs_7_), channel_id=1, source_target_pairs={{0,4},{2,6},{4,0},{6,2},{1,5},{3,7},{5,1},{7,3},{8,12},{10,14},{12... | collective-permute-start | bytes 1769480 | tf_op jit(solution)/shard_map/ppermute | solution.py:534
  32.1 19.4 %collective-permute-start.5 = (bf16[1024,384]{1,0:T(8,128)(2,1)S(1)}, bf16[1024,384]{1,0:T(8,128)(2,1)S(1)}, u32[]{:S(2)}, u32[]{:S(2)}) collective-permute-start(bf16[1024,384]{1,0:T(8,128)(2,1)S(1)} %constant_dynamic-update-slice_fusion.refs_0_), channel_id=1, source_target_pairs={{0,2},{2,0},{4,6},{6,4},{1,3},{3,1},{5,7},{7,5},{8,10},{10,8},{12,... | collective-permute-start | bytes 2359304 | tf_op jit(solution)/shard_map/ppermute | solution.py:534
  51.8 248.0 %all-gather.7.cloned.1.call-start = ((), (), s32[]{:S(2)}) async-start(), calls=%async_computation.1 | async-start | bytes 3981312 | tf_op jit(solution)/shard_map/all_gather | solution.py:710
  66.6 64.0 %collective-permute-start.18 = (bf16[256,384]{1,0:T(8,128)(2,1)}, bf16[256,384]{1,0:T(8,128)(2,1)S(1)}, u32[]{:S(2)}, u32[]{:S(2)}) collective-permute-start(bf16[256,384]{1,0:T(8,128)(2,1)} %get-tuple-element.143), channel_id=1, source_target_pairs={{0,8},{8,16},{16,24},{24,0},{1,9},{9,17},{17,25},{25,1},{2,10},{10... | collective-permute-start | bytes 589832 | tf_op jit(solution)/shard_map/ppermute | solution.py:534
  74.4 56.1 %collective-permute-start.19 = (bf16[256,384]{1,0:T(8,128)(2,1)}, bf16[256,384]{1,0:T(8,128)(2,1)}, u32[]{:S(2)}, u32[]{:S(2)}) collective-permute-start(bf16[256,384]{1,0:T(8,128)(2,1)} %get-tuple-element.144), channel_id=1, source_target_pairs={{0,16},{8,24},{16,0},{24,8},{1,17},{9,25},{17,1},{25,9},{2,18},{10... | collective-permute-start | bytes 589832 | tf_op jit(solution)/shard_map/ppermute | solution.py:534
  74.4 56.1 %collective-permute-start.20 = (bf16[256,384]{1,0:T(8,128)(2,1)}, bf16[256,384]{1,0:T(8,128)(2,1)}, u32[]{:S(2)}, u32[]{:S(2)}) collective-permute-start(bf16[256,384]{1,0:T(8,128)(2,1)} %get-tuple-element.145), channel_id=1, source_target_pairs={{0,24},{8,0},{16,8},{24,16},{1,25},{9,1},{17,9},{25,17},{2,26},{10... | collective-permute-start | bytes 589832 | tf_op jit(solution)/shard_map/ppermute | solution.py:534
  80.3 50.2 %collective-permute-start.21 = (bf16[384,768]{1,0:T(8,128)(2,1)}, bf16[384,768]{1,0:T(8,128)(2,1)S(1)}, u32[]{:S(2)}, u32[]{:S(2)}) collective-permute-start(bf16[384,768]{1,0:T(8,128)(2,1)} %refs_7_), channel_id=1, source_target_pairs={{0,6},{2,4},{4,2},{6,0},{1,7},{3,5},{5,3},{7,1},{8,14},{10,12},{12... | collective-permute-start | bytes 1769480 | tf_op jit(solution)/shard_map/ppermute | solution.py:534
  202.3 44.9 %collective-permute-start.33 = (bf16[1984,384]{1,0:T(8,128)(2,1)S(1)}, bf16[1984,384]{1,0:T(8,128)(2,1)S(1)}, u32[]{:S(2)}, u32[]{:S(2)}) collective-permute-start(bf16[1984,384]{1,0:T(8,128)(2,1)S(1)} %copy-done.2), channel_id=1, source_target_pairs={{0,4},{2,6},{4,0},{6,2},{1,5},{3,7},{5,1},{7,3},{8,12},{10,14},{12... | collective-permute-start | bytes 4571144 | tf_op jit(solution)/shard_map/ppermute | solution.py:534
  203.1 44.1 %collective-permute-start.32 = (bf16[2,384,768]{2,1,0:T(8,128)(2,1)}, bf16[2,384,768]{2,1,0:T(8,128)(2,1)}, u32[]{:S(2)}, u32[]{:S(2)}) collective-permute-start(bf16[2,384,768]{2,1,0:T(8,128)(2,1)} %add_convert_fusion.1), channel_id=1, source_target_pairs={{0,2},{2,0},{4,6},{6,4},{1,3},{3,1},{5,7},{7,5},{8,10},{10,8},{12,... | collective-permute-start | bytes 3538952 | tf_op jit(solution)/shard_map/ppermute | solution.py:534
  206.2 41.0 %collective-permute-start.34 = (bf16[256,384]{1,0:T(8,128)(2,1)}, bf16[256,384]{1,0:T(8,128)(2,1)S(1)}, u32[]{:S(2)}, u32[]{:S(2)}) collective-permute-start(bf16[256,384]{1,0:T(8,128)(2,1)} %get-tuple-element.180), channel_id=1, source_target_pairs={{0,8},{8,16},{16,24},{24,0},{1,9},{9,17},{17,25},{25,1},{2,10},{10... | collective-permute-start | bytes 589832 | tf_op jit(solution)/shard_map/ppermute | solution.py:534
  206.2 41.0 %collective-permute-start.35 = (bf16[256,384]{1,0:T(8,128)(2,1)}, bf16[256,384]{1,0:T(8,128)(2,1)S(1)}, u32[]{:S(2)}, u32[]{:S(2)}) collective-permute-start(bf16[256,384]{1,0:T(8,128)(2,1)} %get-tuple-element.181), channel_id=1, source_target_pairs={{0,16},{8,24},{16,0},{24,8},{1,17},{9,25},{17,1},{25,9},{2,18},{10... | collective-permute-start | bytes 589832 | tf_op jit(solution)/shard_map/ppermute | solution.py:534
  206.2 41.0 %collective-permute-start.36 = (bf16[256,384]{1,0:T(8,128)(2,1)}, bf16[256,384]{1,0:T(8,128)(2,1)S(1)}, u32[]{:S(2)}, u32[]{:S(2)}) collective-permute-start(bf16[256,384]{1,0:T(8,128)(2,1)} %get-tuple-element.182), channel_id=1, source_target_pairs={{0,24},{8,0},{16,8},{24,16},{1,25},{9,1},{17,9},{25,17},{2,26},{10... | collective-permute-start | bytes 589832 | tf_op jit(solution)/shard_map/ppermute | solution.py:534
  249.6 32.4 %collective-permute-start.41 = (bf16[384,768]{1,0:T(8,128)(2,1)S(1)}, bf16[384,768]{1,0:T(8,128)(2,1)S(1)}, u32[]{:S(2)}, u32[]{:S(2)}) collective-permute-start(bf16[384,768]{1,0:T(8,128)(2,1)S(1)} %fusion.3), channel_id=1, source_target_pairs={{0,4},{2,6},{4,0},{6,2},{1,5},{3,7},{5,1},{7,3},{8,12},{10,14},{12... | collective-permute-start | bytes 1769480 | tf_op jit(solution)/shard_map/ppermute | solution.py:534
  251.4 32.5 %collective-permute-start.42 = (bf16[992,384]{1,0:T(8,128)(2,1)S(1)}, bf16[992,384]{1,0:T(8,128)(2,1)}, u32[]{:S(2)}, u32[]{:S(2)}) collective-permute-start(bf16[992,384]{1,0:T(8,128)(2,1)S(1)} %add_convert_fusion.3), channel_id=1, source_target_pairs={{0,2},{2,0},{4,6},{6,4},{1,3},{3,1},{5,7},{7,5},{8,10},{10,8},{12,... | collective-permute-start | bytes 2285576 | tf_op jit(solution)/shard_map/ppermute | solution.py:534
  256.5 27.5 %collective-permute-start.38 = (bf16[256,768]{1,0:T(8,128)(2,1)}, bf16[256,768]{1,0:T(8,128)(2,1)}, u32[]{:S(2)}, u32[]{:S(2)}) collective-permute-start(bf16[256,768]{1,0:T(8,128)(2,1)} %get-tuple-element.192), channel_id=1, source_target_pairs={{0,2},{2,0},{4,6},{6,4},{1,3},{3,1},{5,7},{7,5},{8,10},{10,8},{12,... | collective-permute-start | bytes 1179656 | tf_op jit(solution)/shard_map/ppermute | solution.py:534
  257.8 26.1 %collective-permute-start.39 = (bf16[256,768]{1,0:T(8,128)(2,1)}, bf16[256,768]{1,0:T(8,128)(2,1)}, u32[]{:S(2)}, u32[]{:S(2)}) collective-permute-start(bf16[256,768]{1,0:T(8,128)(2,1)} %get-tuple-element.193), channel_id=1, source_target_pairs={{0,4},{2,6},{4,0},{6,2},{1,5},{3,7},{5,1},{7,3},{8,12},{10,14},{12... | collective-permute-start | bytes 1179656 | tf_op jit(solution)/shard_map/ppermute | solution.py:534
  259.8 29.1 %collective-permute-start.40 = (bf16[256,768]{1,0:T(8,128)(2,1)}, bf16[256,768]{1,0:T(8,128)(2,1)}, u32[]{:S(2)}, u32[]{:S(2)}) collective-permute-start(bf16[256,768]{1,0:T(8,128)(2,1)} %get-tuple-element.194), channel_id=1, source_target_pairs={{0,6},{2,4},{4,2},{6,0},{1,7},{3,5},{5,3},{7,1},{8,14},{10,12},{12... | collective-permute-start | bytes 1179656 | tf_op jit(solution)/shard_map/ppermute | solution.py:534
  290.9 24.2 %collective-permute-start.55 = (bf16[496,384]{1,0:T(8,128)(2,1)S(1)}, bf16[496,384]{1,0:T(8,128)(2,1)S(1)}, u32[]{:S(2)}, u32[]{:S(2)}) collective-permute-start(bf16[496,384]{1,0:T(8,128)(2,1)S(1)} %broadcast_select_fusion.2), channel_id=1, source_target_pairs={{0,8},{8,0},{16,24},{24,16},{1,9},{9,1},{17,25},{25,17},{2,10},{10... | collective-permute-start | bytes 1142792 | tf_op jit(solution)/shard_map/ppermute | solution.py:534
  316.0 20.6 %collective-permute-start.60 = (bf16[192,768]{1,0:T(8,128)(2,1)S(1)}, bf16[192,768]{1,0:T(8,128)(2,1)S(1)}, u32[]{:S(2)}, u32[]{:S(2)}) collective-permute-start(bf16[192,768]{1,0:T(8,128)(2,1)S(1)} %add_convert_fusion.8), channel_id=1, source_target_pairs={{0,8},{8,0},{16,24},{24,16},{1,9},{9,1},{17,25},{25,17},{2,10},{10... | collective-permute-start | bytes 884744 | tf_op jit(solution)/shard_map/ppermute | solution.py:534
  352.6 23.0 %collective-permute-start.48 = (bf16[256,384]{1,0:T(8,128)(2,1)S(1)}, bf16[256,384]{1,0:T(8,128)(2,1)S(1)}, u32[]{:S(2)}, u32[]{:S(2)}) collective-permute-start(bf16[256,384]{1,0:T(8,128)(2,1)S(1)} %copy-done.40), channel_id=1, source_target_pairs={{0,8},{8,16},{16,24},{24,0},{1,9},{9,17},{17,25},{25,1},{2,10},{10... | collective-permute-start | bytes 589832 | tf_op jit(solution)/shard_map/ppermute | solution.py:534
  353.5 23.4 %collective-permute-start.49 = (bf16[256,384]{1,0:T(8,128)(2,1)S(1)}, bf16[256,384]{1,0:T(8,128)(2,1)S(1)}, u32[]{:S(2)}, u32[]{:S(2)}) collective-permute-start(bf16[256,384]{1,0:T(8,128)(2,1)S(1)} %copy-done.39), channel_id=1, source_target_pairs={{0,16},{8,24},{16,0},{24,8},{1,17},{9,25},{17,1},{25,9},{2,18},{10... | collective-permute-start | bytes 589832 | tf_op jit(solution)/shard_map/ppermute | solution.py:534
  355.6 21.3 %collective-permute-start.50 = (bf16[256,384]{1,0:T(8,128)(2,1)S(1)}, bf16[256,384]{1,0:T(8,128)(2,1)S(1)}, u32[]{:S(2)}, u32[]{:S(2)}) collective-permute-start(bf16[256,384]{1,0:T(8,128)(2,1)S(1)} %copy-done.38), channel_id=1, source_target_pairs={{0,24},{8,0},{16,8},{24,16},{1,25},{9,1},{17,9},{25,17},{2,26},{10... | collective-permute-start | bytes 589832 | tf_op jit(solution)/shard_map/ppermute | solution.py:534
  (91 other events, 1000.4 us)
Sparse Core Ops, SparseCore 0:
  51.9 60.6 all-gather.4
  187.0 44.0 all-gather.6
where the time goes:
time: 397 us; the launch traced here: 390 us
  Pallas kernels  182 us (46%)
  starting transfers between devices  83.7 us (21%)
  waiting for transfers between devices  76.7 us (19%)
  other arithmetic  19.1 us (5%)
  between operations  15.3 us (4%)
  local copies, waits for them, and re-layouts  12.6 us (3%)
    ppermute x61, starting transfers between devices, shift(): lax.ppermute(array, axis, [(i, to(i)) for i in range(lax.axis_size(axis))])  83.6 us
    ppermute x61, waiting for transfers between devices, shift(): lax.ppermute(array, axis, [(i, to(i)) for i in range(lax.axis_size(axis))])  76.6 us
    pallas_call x2, Pallas kernels, back(): call(partial(attend_back_kernel, grid_rows, heads, start, seqs, run, bloc...  59.2 us
    pallas_call x1, Pallas kernels, local(): call(partial(attend_kernel, sizes, layout, heads, seqs, run), [((heads, h...  46.6 us
    pallas_call x1, Pallas kernels, local(): call(partial(middle_kernel, plan, grid_rows), [((own_rows, half), BF), ((...  36.2 us
    convert_element_type x13, other arithmetic, add(): return sum((a.astype(F32) for a in arrays)).astype(BF)  12.7 us
    unnamed x118, local copies, waits for them, and re-layouts  10.3 us
  transfers between devices with their start and end apart: 63, of which 18 were waited for; matrix products, arithmetic and copies ran while one was open for 6% of the time, Pallas kernels for 37%

commit v1 on v0

--- a/solution.py
+++ b/solution.py
@@ -166,6 +166,13 @@
     return stop
 
 
+def key_steps(ends, first, run, block, wide, total):
+    low = first_of(ends, first) * block
+    steps = lax.div(last_of(ends, first + run - 1) * block - low + wide - 1, wide)
+    low = jnp.minimum(low, total - steps * wide)
+    return steps, lambda j: pl.ds(pl.multiple_of(low + j * wide, block), wide)
+
+
 def thirds(v):
     one = v.astype(BF)
     rest = v - one.astype(F32)
@@ -180,9 +187,9 @@
     weights = refs[len(layout) : len(layout) + 2]
     bias = refs[len(layout) + 2]
     outs = refs[len(layout) + 3 :]
-    q_ref, k_ref, v_ref, kt_ref, o_ref, xq_ref, own_ref = outs[:7]
-    mixed = outs[7 : 7 + grid_rows]
-    x_ref, score_ref, peak_ref, acc_ref = outs[7 + grid_rows :]
+    q_ref, k_ref, v_ref, o_ref, xq_ref, own_ref = outs[:6]
+    mixed = outs[6 : 6 + grid_rows]
+    x_ref, score_ref, peak_ref, acc_ref = outs[6 + grid_rows :]
     r, c = where[1], where[2]
     ends = sequence_ends(lengths, seqs)
     half = weights[0].shape[1]
@@ -205,8 +212,6 @@
         x0, x1 = x_ref[at, :half], x_ref[at, half:]
         first = 0 if mine else inner
         joined = nt(x0, weights[0][first:, :]) + nt(x1, weights[1][first:, :])
-        flipped = nt(weights[0][inner : 2 * inner, :], x0) + nt(weights[1][inner : 2 * inner, :], x1)
-        kt_ref[:, at] = flipped.astype(BF)
         seg = sequence_of(ends, down + i * run)
         key_tail = jnp.where((lane == seg) | tail_k, 1.0, 0.0)
         for h in range(heads):
@@ -234,23 +239,21 @@
     lane_q = lax.broadcasted_iota(jnp.int32, (rows, LANES), 1)
 
     def one_run(i, carry):
-        first = i * 2 * run + c * run
-        low = lax.div(first_of(ends, first) * block, wide)
-        high = lax.div(last_of(ends, first + run - 1) * block + wide - 1, wide)
+        steps, key_rows = key_steps(ends, i * 2 * run + c * run, run, block, wide, k_ref.shape[1])
         here = rows_at(i, rows)
         peak_ref[...] = jnp.full_like(peak_ref, -3e38)
 
         def score(j, state):
             for h in range(heads):
-                scores = nt(q_ref[h, here, :], k_ref[h, rows_at(j, wide), :])
-                score_ref[h, j - low] = scores
+                scores = nt(q_ref[h, here, :], k_ref[h, key_rows(j), :])
+                score_ref[h, j] = scores
                 peak = peak_ref[h]
                 for t in range(wide // LANES):
                     peak = jnp.maximum(peak, scores[:, t * LANES : (t + 1) * LANES])
                 peak_ref[h] = peak
             return state
 
-        lax.fori_loop(low, high, score, jnp.int32(0))
+        lax.fori_loop(0, steps, score, jnp.int32(0))
         tops = [jnp.max(peak_ref[h], axis=1, keepdims=True) for h in range(heads)]
         for h in range(heads):
             peak_ref[h] = jnp.broadcast_to(tops[h], (rows, LANES))
@@ -259,11 +262,11 @@
         def mix(j, state):
             for h in range(heads):
                 peak = jnp.concatenate([peak_ref[h]] * (wide // LANES), axis=1)
-                part = jnp.exp(score_ref[h, j - low] - peak).astype(BF)
-                acc_ref[h] += nn(part, v_ref[h, rows_at(j, wide), :])
+                part = jnp.exp(score_ref[h, j] - peak).astype(BF)
+                acc_ref[h] += nn(part, v_ref[h, key_rows(j), :])
             return state
 
-        lax.fori_loop(low, high, mix, jnp.int32(0))
+        lax.fori_loop(0, steps, mix, jnp.int32(0))
         for h in range(heads):
             acc = acc_ref[h]
             total = acc[:, HEAD : HEAD + 1]
@@ -283,7 +286,7 @@
 
 
 def attend_back_kernel(
-    grid_rows, heads_all, start, seqs, run, block, where, lengths, q_ref, k_ref, v_ref, kt_ref, o_ref, *refs
+    grid_rows, heads_all, start, seqs, run, block, where, lengths, q_ref, k_ref, v_ref, o_ref, *refs
 ):
     grads = refs[:grid_rows]
     dq_ref, own_ref, other_ref, do_ref, query_acc, key_acc, value_acc = refs[grid_rows:]
@@ -310,26 +313,25 @@
     value_acc[...] = jnp.zeros_like(value_acc)
 
     def one_run(i, carry):
-        first = i * 2 * run + c * run
-        low = lax.div(first_of(ends, first) * block, wide)
-        high = lax.div(last_of(ends, first + run - 1) * block + wide - 1, wide)
+        steps, key_rows = key_steps(ends, i * 2 * run + c * run, run, block, wide, k_ref.shape[1])
         here = rows_at(i, rows)
         query_acc[...] = jnp.zeros_like(query_acc)
 
         def keys(j, state):
-            at = rows_at(j, wide)
+            at = key_rows(j)
             for h in range(heads):
                 query, grad = q_ref[h, here, :], do_ref[h, here, :]
-                shares = jnp.exp(nt(k_ref[h, at, :], query))
+                key = k_ref[h, at, :]
+                shares = jnp.exp(nt(key, query))
                 score_grads = (shares * nt(v_ref[h, at, :], grad)).astype(BF)
                 value_acc[h, at, :] += nn(shares.astype(BF), grad)
                 key_acc[h, at, :] += nn(score_grads, query)
-                query_acc[h] += nn(kt_ref[h * HEAD : (h + 1) * HEAD, at], score_grads)
+                query_acc[h] += tn(score_grads, key)
             return state
 
-        lax.fori_loop(low, high, keys, jnp.int32(0))
+        lax.fori_loop(0, steps, keys, jnp.int32(0))
         for h in range(heads):
-            dq_ref[h, here, :] = (query_acc[h].T * (HEAD**-0.5)).astype(BF)
+            dq_ref[h, here, :] = (query_acc[h, :, :HEAD] * (HEAD**-0.5)).astype(BF)
         return carry
 
     lax.fori_loop(0, local_runs, one_run, jnp.int32(0))
@@ -567,14 +569,15 @@
     return add(own[2:], got[2:])
 
 
-def reduce_groups(array, group):
+def reduce_groups(array, group, second=(), third=()):
     if lax.axis_size("tok") != 4:
         return lax.psum(array, "tok")
     side = (group ^ (group >> 1)) & 1
     middle = array.shape[0] // 2
     low, high = array[:middle], array[middle:]
     half = add(jnp.where(side == 0, low, high), shift(jnp.where(side == 0, high, low), "tok", lambda i: i ^ 1))
-    half = add(half, shift(half, "tok", lambda i: i ^ 3))
+    half = after(half, *second)
+    half = add(after(half, *third), shift(half, "tok", lambda i: i ^ 3))
     rest = shift(half, "tok", lambda i: i ^ 1)
     return jnp.concatenate([jnp.where(side == 0, half, rest), jnp.where(side == 0, rest, half)], axis=0)
 
@@ -652,7 +655,8 @@
     chunk = jnp.concatenate(after_all(got, place, *first_near), axis=0)
     chunk_near = gather_near(chunk)
     dy_sent = call(partial(send_again_kernel, sizes), [(piece, BF)] * groups, "sv")(table, after(cotangent, *got))
-    chunk_near = after_all(chunk_near, *dy_sent)
+    dy_got = exchange(dy_sent)
+    chunk_near = after_all(chunk_near, *dy_got)
     layout, pieces = [], []
     parts = gather_row(chunk, *chunk_near, shard_rows // 2)
     for k, top, part in parts:
@@ -664,15 +668,13 @@
     first_all = [part for weight in first_row for part in (weight, to_col(weight))]
     pieces[0] = after(pieces[0], *first_all)
     first_far = to_row(after(up_weight, *far), 3)
-    dy_got = exchange(after_all(dy_sent, *far))
     wide_keys = 2 * rows
-    q, k, v, kt, mixed_own, xq, x_own, *mixed = call(
+    q, k, v, mixed_own, xq, x_own, *mixed = call(
         partial(attend_kernel, sizes, layout, heads, seqs, run),
         [
             ((heads, half_rows, LANES), BF),
             ((heads, 2 * half_rows, LANES), BF),
             ((heads, 2 * half_rows, LANES), BF),
-            ((inner, 2 * half_rows), BF),
             ((heads, half_rows, HEAD), BF),
             ((half_rows, width), BF),
             ((own_rows, width), BF),
@@ -688,7 +690,8 @@
         us=47,
     )(place, where, lengths, *pieces, joined_weight, to_col(joined_weight), project_bias)
 
-    mixed = after_all(mixed, *dy_got, first_far)
+    mixed = after_all(mixed, first_far)
+    dy_got[0] = after(dy_got[0], mixed[0])
     first_far = after(first_far, mixed[0])
     first_all += [first_far, to_col(first_far)]
     dy_own, dy_other = call(
@@ -747,8 +750,7 @@
             2: ((number, half_rows, LANES), start // number),
             3: ((number, 2 * half_rows, LANES), start // number),
             4: ((number, 2 * half_rows, LANES), start // number),
-            5: ((number * HEAD, 2 * half_rows), start // number),
-            6: ((number, half_rows, HEAD), start // number),
+            5: ((number, half_rows, HEAD), start // number),
         }
         return call(
             partial(attend_back_kernel, grid_rows, heads, start, seqs, run, block),
@@ -757,16 +759,16 @@
                 ((number, half_rows, LANES), F32),
                 ((number, half_rows, LANES), BF),
             ],
-            "ss" + "v" * (5 + grid_rows),
+            "ss" + "v" * (4 + grid_rows),
             [
                 pltpu.VMEM((number, half_rows, LANES), BF),
-                pltpu.VMEM((number, HEAD, rows), F32),
+                pltpu.VMEM((number, rows, LANES), F32),
                 pltpu.VMEM((number, 2 * half_rows, LANES), F32),
                 pltpu.VMEM((number, 2 * half_rows, LANES), F32),
             ],
             us=16 * number,
             blocks=held,
-        )(where, lengths, q, k, v, kt, mixed_own, *grads)
+        )(where, lengths, q, k, v, mixed_own, *grads)
 
     def join(dq, own, got):
         number = dq.shape[0]
@@ -794,18 +796,19 @@
     second_sum = add(second_own[second_cut[0]], second_got[second_cut[0]], second_came[:second_rows], second_last)
     kv_got = after(to_col(kv_other), first_sum, second_sum)
     last_got, leaving, last_joined = join(dq, kv_own, kv_got)
-    first_sum, second_sum = reduce_groups(first_sum, group), reduce_groups(second_sum, group)
     output = come_back(out_got)
+    in_own, in_other = call(project_in_grad_kernel, [((wide + 32, half), BF)] * 2, "vvv", us=6)(joined, last_joined, xq)
+    in_got = to_col(in_other)
+    last_got[0] = after(last_got[0], in_own)
     dx_own, dx_other = call(
         partial(input_grad_kernel, grid_rows, 2), [((own_rows, half), BF)] * 2, "s" + "v" * (2 * grid_rows + 2), us=7
     )(where, *joined_got, *last_got, joined_all, grad_one)
     dx_pieces = leave(dx_own, to_col(dx_other))
-    in_own, in_other = call(project_in_grad_kernel, [((wide + 32, half), BF)] * 2, "vvv", us=6)(
-        joined, after(last_joined, *dx_pieces), xq
-    )
-    in_sum = reduce_groups(add(in_own, to_col(in_other)), group)
+    first_sum = reduce_groups(first_sum, group, (last_joined,), dx_pieces)
+    second_sum = reduce_groups(second_sum, group, (last_joined,), dx_pieces)
     dx_got = exchange(dx_pieces)
     input_grad = come_back(dx_got)
+    in_sum = reduce_groups(add(in_own, in_got), group, dx_pieces)
 
     tops = [sum(spans[:i]) for i in range(6)]
     in_parts = [in_sum[top : top + span] for top, span in zip(tops, spans)]

time: 397 us -> 387 us (0.975)
  waiting for transfers between devices: 76.7 us -> 61.2 us
  starting transfers between devices: 83.7 us -> 92.4 us
  Pallas kernels: 182 us -> 175 us
  local copies, waits for them, and re-layouts: 12.6 us -> 17.4 us
    ppermute x61, waiting for transfers between devices: 76.6 us -> 61.2 us  [shift(): lax.ppermute(array, axis, [(i, to(i)) for i in range(lax.axis_size(axis))])]
    ppermute x61, starting transfers between devices: 83.6 us -> 92.4 us  [shift(): lax.ppermute(array, axis, [(i, to(i)) for i in range(lax.axis_size(axis))])]
    pallas_call x1, Pallas kernels: 46.6 us -> 41.5 us  [local(): call(partial(attend_kernel, sizes, layout, heads, seqs, run), [((heads, h...]
    unnamed x118 -> x110, local copies, waits for them, and re-layouts: 10.3 us -> 15.2 us
  transfers between devices with their start and end apart: 63 -> 63, of which waited for: 18 -> 17; matrix products, arithmetic and copies ran while one was open for 6% -> 7% of each run, Pallas kernels for 37% -> 37%
where the time goes in v1:
time: 387 us; the launch traced here: 381 us
  Pallas kernels  175 us (45%)
  starting transfers between devices  92.4 us (24%)
  waiting for transfers between devices  61.2 us (16%)
  other arithmetic  19.2 us (5%)
  local copies, waits for them, and re-layouts  17.4 us (4%)
  between operations  15.2 us (4%)
    ppermute x61, starting transfers between devices, shift(): lax.ppermute(array, axis, [(i, to(i)) for i in range(lax.axis_size(axis))])  92.4 us
    ppermute x61, waiting for transfers between devices, shift(): lax.ppermute(array, axis, [(i, to(i)) for i in range(lax.axis_size(axis))])  61.2 us
    pallas_call x2, Pallas kernels, back(): call(partial(attend_back_kernel, grid_rows, heads, start, seqs, run, bloc...  57 us
    pallas_call x1, Pallas kernels, local(): call(partial(attend_kernel, sizes, layout, heads, seqs, run), [((heads, h...  41.5 us
    pallas_call x1, Pallas kernels, local(): call(partial(middle_kernel, plan, grid_rows), [((own_rows, half), BF), ((...  36.2 us
    unnamed x110, local copies, waits for them, and re-layouts  15.2 us
    convert_element_type x13, other arithmetic, add(): return sum((a.astype(F32) for a in arrays)).astype(BF)  12.8 us
  transfers between devices with their start and end apart: 63, of which 17 were waited for; matrix products, arithmetic and copies ran while one was open for 7% of the time, Pallas kernels for 37%

profile of v1, /device:TPU:0, one launch (start us, length us, event | category | flops | bytes accessed | tf_op | source)
XLA Modules:
  0.0 380.7 jit_solution(8418230131939097986)
XLA Ops:
  7.2 3.0 collective-permute-start.3
  12.3 2.8 shard_map.263
  25.2 6.7 %collective-permute-done.1 = bf16[256,384]{1,0:T(8,128)(2,1)S(1)} collective-permute-done((bf16[256,384]{1,0:T(8,128)(2,1)}, bf16[256,384]{1,0:T(8,128)(2,1)S(1)}, u32[]{:S(2)}, u32[]{:S(2)}) %collective-permute-start.1) | collective-permute-done | bytes 196640 | tf_op jit(solution)/shard_map/ppermute | solution.py:536
  35.3 4.7 %collective-permute-start.7 = (bf16[256,384]{1,0:T(8,128)(2,1)}, bf16[256,384]{1,0:T(8,128)(2,1)}, u32[]{:S(2)}, u32[]{:S(2)}) collective-permute-start(bf16[256,384]{1,0:T(8,128)(2,1)} %get-tuple-element.130), channel_id=1, source_target_pairs={{0,8},{8,16},{16,24},{24,0},{1,9},{9,17},{17,25},{25,1},{2,10},{10... | collective-permute-start | bytes 589832 | tf_op jit(solution)/shard_map/ppermute | solution.py:536
  48.1 5.3 %collective-permute-done.8.refs_2_ = bf16[256,384]{1,0:T(8,128)(2,1)} collective-permute-done((bf16[256,384]{1,0:T(8,128)(2,1)}, bf16[256,384]{1,0:T(8,128)(2,1)}, u32[]{:S(2)}, u32[]{:S(2)}) %collective-permute-start.8) | collective-permute-done | bytes 196640 | tf_op jit(solution)/shard_map/ppermute | solution.py:536
  57.8 7.5 %collective-permute-done.16.refs_6_ = bf16[512,384]{1,0:T(8,128)(2,1)S(1)} collective-permute-done((bf16[512,384]{1,0:T(8,128)(2,1)S(1)}, bf16[512,384]{1,0:T(8,128)(2,1)S(1)}, u32[]{:S(2)}, u32[]{:S(2)}) %collective-permute-start.16) | collective-permute-done | bytes 393248 | tf_op jit(solution)/shard_map/ppermute | solution.py:536
  72.8 41.5 %shard_map.266 = (bf16[3,2048,128]{2,1,0:T(8,128)(2,1)}, bf16[3,4096,128]{2,1,0:T(8,128)(2,1)}, bf16[3,4096,128]{2,1,0:T(8,128)(2,1)}, bf16[3,2048,64]{2,1,0:T(8...) custom-call(s32[128]{0:T(128)} %shard_map.264.place, ...), custom_call_target="tpu_custom_call" | custom-call | flops 14099999744 | bytes 47000000 | tf_op jit(solution)/shard_map/pallas_call | solution.py:672
  120.9 4.2 %collective-permute-done.22.refs_1_ = bf16[256,384]{1,0:T(8,128)(2,1)S(1)} collective-permute-done((bf16[256,384]{1,0:T(8,128)(2,1)S(1)}, bf16[256,384]{1,0:T(8,128)(2,1)S(1)}, u32[]{:S(2)}, u32[]{:S(2)}) %collective-permute-start.22) | collective-permute-done | bytes 196640 | tf_op jit(solution)/shard_map/ppermute | solution.py:536
  125.1 4.9 %collective-permute-done.23.refs_2_ = bf16[256,384]{1,0:T(8,128)(2,1)S(1)} collective-permute-done((bf16[256,384]{1,0:T(8,128)(2,1)S(1)}, bf16[256,384]{1,0:T(8,128)(2,1)S(1)}, u32[]{:S(2)}, u32[]{:S(2)}) %collective-permute-start.23) | collective-permute-done | bytes 196640 | tf_op jit(solution)/shard_map/ppermute | solution.py:536
  131.1 36.2 %shard_map.268 = (bf16[512,384]{1,0:T(8,128)(2,1)}, f32[512,768]{1,0:T(8,128)}, bf16[256,384]{1,0:T(8,128)(2,1)}, bf16[256,384]{1,0:T(8,128)(2,1)}, bf16[256,384...) custom-call(s32[3]{0:T(128)} %pad_add_fusion.where, ...), custom_call_target="tpu_custom_call" | custom-call | flops 12600000512 | bytes 42000000 | tf_op jit(solution)/shard_map/pallas_call | solution.py:716
  176.8 3.1 add_convert_fusion.1
  182.1 3.3 shard_map.269
  187.3 12.1 %collective-permute-start.34 = (bf16[256,384]{1,0:T(8,128)(2,1)}, bf16[256,384]{1,0:T(8,128)(2,1)S(1)}, u32[]{:S(2)}, u32[]{:S(2)}) collective-permute-start(bf16[256,384]{1,0:T(8,128)(2,1)} %get-tuple-element.177), channel_id=1, source_target_pairs={{0,8},{8,16},{16,24},{24,0},{1,9},{9,17},{17,25},{25,1},{2,10},{10... | collective-permute-start | bytes 589832 | tf_op jit(solution)/shard_map/ppermute | solution.py:536
  201.8 35.5 %shard_map.270 = (bf16[2,2048,64]{2,1,0:T(8,128)(2,1)}, f32[2,2048,128]{2,1,0:T(8,128)}, bf16[2,2048,128]{2,1,0:T(8,128)(2,1)}) custom-call(s32[3]{0:T(128)} %pad_add_fusion.where, s32[1,4]{1,0:T(1,128)} %lengths.5, bf16[3,2048,128]{2,1,0:T(8,128)(2,1)} %get-tuple-element.171.q_ref, bf16[3,4096,128]{2,1,0:T(8,128)(2,1)} %get-tuple-element.172.k_ref, ...), custom_call_target="tpu_custom_call" | custom-call | flops 9600000000 | bytes 32000000 | tf_op jit(solution)/shard_map/pallas_call | solution.py:755
  244.0 4.3 %shard_map.271 = (bf16[256,768]{1,0:T(8,128)(2,1)}, bf16[256,768]{1,0:T(8,128)(2,1)}, bf16[256,768]{1,0:T(8,128)(2,1)}, bf16[256,768]{1,0:T(8,128)(2,1)}, bf16[2048,384]{1,0:T(8,128)(2,1)}) custom-call(s32[3]{0:T(128)} %pad_add_fusion.where, bf16[2,2048,64]{2,1,0:T(8,128)(2,1)} %get-tuple-element.181.dq_ref, f32[2,2048,128]{2,1,0:T(8,128)} %get-tuple-element.185.own_ref, ...), custom_call_target="tpu_custom_call" | custom-call | flops 1200000000 | bytes 4000000 | tf_op jit(solution)/shard_map/pallas_call | solution.py:775
  251.8 21.5 %shard_map.272 = (bf16[1,2048,64]{2,1,0:T(8,128)(2,1)}, f32[1,2048,128]{2,1,0:T(8,128)}, bf16[1,2048,128]{2,1,0:T(8,128)(2,1)}) custom-call(s32[3]{0:T(128)} %pad_add_fusion.where, s32[1,4]{1,0:T(1,128)} %lengths.5, bf16[3,2048,128]{2,1,0:T(8,128)(2,1)} %get-tuple-element.171.q_ref, bf16[3,4096,128]{2,1,0:T(8,128)(2,1)} %get-tuple-element.172.k_ref, ...), custom_call_target="tpu_custom_call" | custom-call | flops 4800000000 | bytes 16000000 | tf_op jit(solution)/shard_map/pallas_call | solution.py:755
  281.4 3.6 collective-permute-start.55
  288.1 3.0 shard_map.274
  291.0 6.6 %shard_map.275 = (bf16[608,384]{1,0:T(8,128)(2,1)}, bf16[608,384]{1,0:T(8,128)(2,1)}) custom-call(bf16[2048,384]{1,0:T(8,128)(2,1)} %get-tuple-element.202.refs_0_, bf16[2048,192]{1,0:T(8,128)(2,1)} %get-tuple-element.203.refs_1_, bf16[2048,768]{1,0:T(8,128)(2,1)} %get-tuple-element.204.refs_2_), custom_call_target="tpu_custom_call" | custom-call | flops 1800000000 | bytes 6000000 | tf_op jit(solution)/shard_map/pallas_call | solution.py:800
  310.4 7.1 %shard_map.276 = (bf16[512,384]{1,0:T(8,128)(2,1)}, bf16[512,384]{1,0:T(8,128)(2,1)}) custom-call(s32[3]{0:T(128)} %pad_add_fusion.where, bf16[256,768]{1,0:T(8,128)(2,1)} %get-tuple-element.188.refs_0_, bf16[256,768]{1,0:T(8,128)(2,1)} %collective-permute-done.38.refs_1_, bf16[256,768]{1,0:T(8,128)(2,1)} %collective-permute-done.39.refs_2_, ...), custom_call_target="tpu_custom_call" | custom-call | flops 2100000000 | bytes 7000000 | tf_op jit(solution)/shard_map/pallas_call | solution.py:803
  322.8 3.1 collective-permute-start.49
  327.3 15.8 %collective-permute-start.57 = (bf16[496,384]{1,0:T(8,128)(2,1)S(1)}, bf16[496,384]{1,0:T(8,128)(2,1)S(1)}, u32[]{:S(2)}, u32[]{:S(2)}) collective-permute-start(bf16[496,384]{1,0:T(8,128)(2,1)S(1)} %add_convert_fusion.6), channel_id=1, source_target_pairs={{0,8},{8,0},{16,24},{24,16},{1,9},{9,1},{17,25},{25,17},{2,10},{10... | collective-permute-start | bytes 1142792 | tf_op jit(solution)/shard_map/ppermute | solution.py:536
  350.2 13.7 %collective-permute-done.60 = bf16[192,768]{1,0:T(8,128)(2,1)S(1)} collective-permute-done((bf16[192,768]{1,0:T(8,128)(2,1)S(1)}, bf16[192,768]{1,0:T(8,128)(2,1)S(1)}, u32[]{:S(2)}, u32[]{:S(2)}) %collective-permute-start.60) | collective-permute-done | bytes 294944 | tf_op jit(solution)/shard_map/ppermute | solution.py:536
  368.4 3.3 collective-permute-done.54
  (278 shorter events, 112.9 us)
Async XLA Ops:
  7.2 122.9 %all-gather.5.cloned.1.call-start = ((), (), s32[]{:S(2)}) async-start(), calls=%async_computation | async-start | bytes 6746112 | tf_op jit(solution)/shard_map/all_gather | solution.py:666
  7.2 24.7 %collective-permute-start.3 = (bf16[384,768]{1,0:T(8,128)(2,1)}, bf16[384,768]{1,0:T(8,128)(2,1)}, u32[]{:S(2)}, u32[]{:S(2)}) collective-permute-start(bf16[384,768]{1,0:T(8,128)(2,1)} %refs_7_), channel_id=1, source_target_pairs={{0,2},{2,0},{4,6},{6,4},{1,3},{3,1},{5,7},{7,5},{8,10},{10,8},{12,... | collective-permute-start | bytes 1769480 | tf_op jit(solution)/shard_map/ppermute | solution.py:536
  10.2 21.7 %collective-permute-start.4 = (bf16[384,768]{1,0:T(8,128)(2,1)}, bf16[384,768]{1,0:T(8,128)(2,1)}, u32[]{:S(2)}, u32[]{:S(2)}) collective-permute-start(bf16[384,768]{1,0:T(8,128)(2,1)} %refs_7_), channel_id=1, source_target_pairs={{0,4},{2,6},{4,0},{6,2},{1,5},{3,7},{5,1},{7,3},{8,12},{10,14},{12... | collective-permute-start | bytes 1769480 | tf_op jit(solution)/shard_map/ppermute | solution.py:536
  32.1 21.3 %collective-permute-start.5 = (bf16[1024,384]{1,0:T(8,128)(2,1)S(1)}, bf16[1024,384]{1,0:T(8,128)(2,1)S(1)}, u32[]{:S(2)}, u32[]{:S(2)}) collective-permute-start(bf16[1024,384]{1,0:T(8,128)(2,1)S(1)} %constant_dynamic-update-slice_fusion.refs_0_), channel_id=1, source_target_pairs={{0,2},{2,0},{4,6},{6,4},{1,3},{3,1},{5,7},{7,5},{8,10},{10,8},{12,... | collective-permute-start | bytes 2359304 | tf_op jit(solution)/shard_map/ppermute | solution.py:536
  53.4 254.1 %all-gather.7.cloned.1.call-start = ((), (), s32[]{:S(2)}) async-start(), calls=%async_computation.1 | async-start | bytes 3981312 | tf_op jit(solution)/shard_map/all_gather | solution.py:713
  67.7 46.7 %collective-permute-start.21 = (bf16[384,768]{1,0:T(8,128)(2,1)}, bf16[384,768]{1,0:T(8,128)(2,1)S(1)}, u32[]{:S(2)}, u32[]{:S(2)}) collective-permute-start(bf16[384,768]{1,0:T(8,128)(2,1)} %refs_7_), channel_id=1, source_target_pairs={{0,6},{2,4},{4,2},{6,0},{1,7},{3,5},{5,3},{7,1},{8,14},{10,12},{12... | collective-permute-start | bytes 1769480 | tf_op jit(solution)/shard_map/ppermute | solution.py:536
  185.5 52.6 %collective-permute-start.33 = (bf16[1984,384]{1,0:T(8,128)(2,1)}, bf16[1984,384]{1,0:T(8,128)(2,1)}, u32[]{:S(2)}, u32[]{:S(2)}) collective-permute-start(bf16[1984,384]{1,0:T(8,128)(2,1)} %add_convert_fusion), channel_id=1, source_target_pairs={{0,4},{2,6},{4,0},{6,2},{1,5},{3,7},{5,1},{7,3},{8,12},{10,14},{12... | collective-permute-start | bytes 4571144 | tf_op jit(solution)/shard_map/ppermute | solution.py:536
  186.9 50.5 %collective-permute-start.32 = (bf16[2,384,768]{2,1,0:T(8,128)(2,1)S(1)}, bf16[2,384,768]{2,1,0:T(8,128)(2,1)}, u32[]{:S(2)}, u32[]{:S(2)}) collective-permute-start(bf16[2,384,768]{2,1,0:T(8,128)(2,1)S(1)} %copy-done.3), channel_id=1, source_target_pairs={{0,2},{2,0},{4,6},{6,4},{1,3},{3,1},{5,7},{7,5},{8,10},{10,8},{12,... | collective-permute-start | bytes 3538952 | tf_op jit(solution)/shard_map/ppermute | solution.py:536
  187.3 50.0 %collective-permute-start.34 = (bf16[256,384]{1,0:T(8,128)(2,1)}, bf16[256,384]{1,0:T(8,128)(2,1)S(1)}, u32[]{:S(2)}, u32[]{:S(2)}) collective-permute-start(bf16[256,384]{1,0:T(8,128)(2,1)} %get-tuple-element.177), channel_id=1, source_target_pairs={{0,8},{8,16},{16,24},{24,0},{1,9},{9,17},{17,25},{25,1},{2,10},{10... | collective-permute-start | bytes 589832 | tf_op jit(solution)/shard_map/ppermute | solution.py:536
  199.5 37.9 %collective-permute-start.35 = (bf16[256,384]{1,0:T(8,128)(2,1)}, bf16[256,384]{1,0:T(8,128)(2,1)S(1)}, u32[]{:S(2)}, u32[]{:S(2)}) collective-permute-start(bf16[256,384]{1,0:T(8,128)(2,1)} %get-tuple-element.178), channel_id=1, source_target_pairs={{0,16},{8,24},{16,0},{24,8},{1,17},{9,25},{17,1},{25,9},{2,18},{10... | collective-permute-start | bytes 589832 | tf_op jit(solution)/shard_map/ppermute | solution.py:536
  199.5 37.9 %collective-permute-start.36 = (bf16[256,384]{1,0:T(8,128)(2,1)}, bf16[256,384]{1,0:T(8,128)(2,1)}, u32[]{:S(2)}, u32[]{:S(2)}) collective-permute-start(bf16[256,384]{1,0:T(8,128)(2,1)} %get-tuple-element.179), channel_id=1, source_target_pairs={{0,24},{8,0},{16,8},{24,16},{1,25},{9,1},{17,9},{25,17},{2,26},{10... | collective-permute-start | bytes 589832 | tf_op jit(solution)/shard_map/ppermute | solution.py:536
  239.6 33.7 %collective-permute-start.41 = (bf16[384,768]{1,0:T(8,128)(2,1)S(1)}, bf16[384,768]{1,0:T(8,128)(2,1)}, u32[]{:S(2)}, u32[]{:S(2)}) collective-permute-start(bf16[384,768]{1,0:T(8,128)(2,1)S(1)} %fusion.3), channel_id=1, source_target_pairs={{0,4},{2,6},{4,0},{6,2},{1,5},{3,7},{5,1},{7,3},{8,12},{10,14},{12... | collective-permute-start | bytes 1769480 | tf_op jit(solution)/shard_map/ppermute | solution.py:536
  242.7 34.7 %collective-permute-start.42 = (bf16[992,384]{1,0:T(8,128)(2,1)S(1)}, bf16[992,384]{1,0:T(8,128)(2,1)}, u32[]{:S(2)}, u32[]{:S(2)}) collective-permute-start(bf16[992,384]{1,0:T(8,128)(2,1)S(1)} %add_convert_fusion.3), channel_id=1, source_target_pairs={{0,2},{2,0},{4,6},{6,4},{1,3},{3,1},{5,7},{7,5},{8,10},{10,8},{12,... | collective-permute-start | bytes 2285576 | tf_op jit(solution)/shard_map/ppermute | solution.py:536
  248.3 29.2 %collective-permute-start.38 = (bf16[256,768]{1,0:T(8,128)(2,1)}, bf16[256,768]{1,0:T(8,128)(2,1)}, u32[]{:S(2)}, u32[]{:S(2)}) collective-permute-start(bf16[256,768]{1,0:T(8,128)(2,1)} %get-tuple-element.189), channel_id=1, source_target_pairs={{0,2},{2,0},{4,6},{6,4},{1,3},{3,1},{5,7},{7,5},{8,10},{10,8},{12,... | collective-permute-start | bytes 1179656 | tf_op jit(solution)/shard_map/ppermute | solution.py:536
  249.1 28.3 %collective-permute-start.39 = (bf16[256,768]{1,0:T(8,128)(2,1)}, bf16[256,768]{1,0:T(8,128)(2,1)}, u32[]{:S(2)}, u32[]{:S(2)}) collective-permute-start(bf16[256,768]{1,0:T(8,128)(2,1)} %get-tuple-element.190), channel_id=1, source_target_pairs={{0,4},{2,6},{4,0},{6,2},{1,5},{3,7},{5,1},{7,3},{8,12},{10,14},{12... | collective-permute-start | bytes 1179656 | tf_op jit(solution)/shard_map/ppermute | solution.py:536
  249.9 29.3 %collective-permute-start.40 = (bf16[256,768]{1,0:T(8,128)(2,1)}, bf16[256,768]{1,0:T(8,128)(2,1)}, u32[]{:S(2)}, u32[]{:S(2)}) collective-permute-start(bf16[256,768]{1,0:T(8,128)(2,1)} %get-tuple-element.191), channel_id=1, source_target_pairs={{0,6},{2,4},{4,2},{6,0},{1,7},{3,5},{5,3},{7,1},{8,14},{10,12},{12... | collective-permute-start | bytes 1179656 | tf_op jit(solution)/shard_map/ppermute | solution.py:536
  275.0 22.8 %collective-permute-start.58 = (bf16[192,768]{1,0:T(8,128)(2,1)S(1)}, bf16[192,768]{1,0:T(8,128)(2,1)S(1)}, u32[]{:S(2)}, u32[]{:S(2)}) collective-permute-start(bf16[192,768]{1,0:T(8,128)(2,1)S(1)} %broadcast_select_fusion.5), channel_id=1, source_target_pairs={{0,8},{8,0},{16,24},{24,16},{1,9},{9,1},{17,25},{25,17},{2,10},{10... | collective-permute-start | bytes 884744 | tf_op jit(solution)/shard_map/ppermute | solution.py:536
  301.7 24.2 %collective-permute-start.56 = (bf16[496,384]{1,0:T(8,128)(2,1)S(1)}, bf16[496,384]{1,0:T(8,128)(2,1)S(1)}, u32[]{:S(2)}, u32[]{:S(2)}) collective-permute-start(bf16[496,384]{1,0:T(8,128)(2,1)S(1)} %add_convert_fusion.7), channel_id=1, source_target_pairs={{0,24},{8,16},{16,8},{24,0},{1,25},{9,17},{17,9},{25,1},{2,26},{10... | collective-permute-start | bytes 1142792 | tf_op jit(solution)/shard_map/ppermute | solution.py:536
  305.7 21.5 %collective-permute-start.59 = (bf16[192,768]{1,0:T(8,128)(2,1)S(1)}, bf16[192,768]{1,0:T(8,128)(2,1)S(1)}, u32[]{:S(2)}, u32[]{:S(2)}) collective-permute-start(bf16[192,768]{1,0:T(8,128)(2,1)S(1)} %add_convert_fusion.9), channel_id=1, source_target_pairs={{0,24},{8,16},{16,8},{24,0},{1,25},{9,17},{17,9},{25,1},{2,26},{10... | collective-permute-start | bytes 884744 | tf_op jit(solution)/shard_map/ppermute | solution.py:536
  317.7 25.4 %collective-permute-start.52 = (bf16[304,384]{1,0:T(8,128)(2,1)S(1)}, bf16[304,384]{1,0:T(8,128)(2,1)S(1)}, u32[]{:S(2)}, u32[]{:S(2)}) collective-permute-start(bf16[304,384]{1,0:T(8,128)(2,1)S(1)} %broadcast_select_fusion.8), channel_id=1, source_target_pairs={{0,8},{8,0},{16,24},{24,16},{1,9},{9,1},{17,25},{25,17},{2,10},{10... | collective-permute-start | bytes 700424 | tf_op jit(solution)/shard_map/ppermute | solution.py:536
  322.5 20.8 %collective-permute-start.48 = (bf16[256,384]{1,0:T(8,128)(2,1)}, bf16[256,384]{1,0:T(8,128)(2,1)S(1)}, u32[]{:S(2)}, u32[]{:S(2)}) collective-permute-start(bf16[256,384]{1,0:T(8,128)(2,1)} %get-tuple-element.215), channel_id=1, source_target_pairs={{0,8},{8,16},{16,24},{24,0},{1,9},{9,17},{17,25},{25,1},{2,10},{10... | collective-permute-start | bytes 589832 | tf_op jit(solution)/shard_map/ppermute | solution.py:536
  322.8 23.9 %collective-permute-start.49 = (bf16[256,384]{1,0:T(8,128)(2,1)}, bf16[256,384]{1,0:T(8,128)(2,1)S(1)}, u32[]{:S(2)}, u32[]{:S(2)}) collective-permute-start(bf16[256,384]{1,0:T(8,128)(2,1)} %get-tuple-element.216), channel_id=1, source_target_pairs={{0,16},{8,24},{16,0},{24,8},{1,17},{9,25},{17,1},{25,9},{2,18},{10... | collective-permute-start | bytes 589832 | tf_op jit(solution)/shard_map/ppermute | solution.py:536
  327.3 37.9 %collective-permute-start.57 = (bf16[496,384]{1,0:T(8,128)(2,1)S(1)}, bf16[496,384]{1,0:T(8,128)(2,1)S(1)}, u32[]{:S(2)}, u32[]{:S(2)}) collective-permute-start(bf16[496,384]{1,0:T(8,128)(2,1)S(1)} %add_convert_fusion.6), channel_id=1, source_target_pairs={{0,8},{8,0},{16,24},{24,16},{1,9},{9,1},{17,25},{25,17},{2,10},{10... | collective-permute-start | bytes 1142792 | tf_op jit(solution)/shard_map/ppermute | solution.py:536
  343.3 21.7 %collective-permute-start.53 = (bf16[304,384]{1,0:T(8,128)(2,1)S(1)}, bf16[304,384]{1,0:T(8,128)(2,1)S(1)}, u32[]{:S(2)}, u32[]{:S(2)}) collective-permute-start(bf16[304,384]{1,0:T(8,128)(2,1)S(1)} %add_convert_fusion.11), channel_id=1, source_target_pairs={{0,24},{8,16},{16,8},{24,0},{1,25},{9,17},{17,9},{25,1},{2,26},{10... | collective-permute-start | bytes 700424 | tf_op jit(solution)/shard_map/ppermute | solution.py:536
  (87 other events, 810.2 us)
Sparse Core Ops, SparseCore 0:
  53.6 60.0 all-gather.4
  171.8 52.5 all-gather.6

commit v2 on v1

--- a/solution.py
+++ b/solution.py
@@ -366,21 +366,26 @@
         pieces[k][...] = jnp.concatenate(cells, axis=1)
 
 
-def project_in_grad_kernel(*refs):
+def project_in_grad_kernel(parts, heads, *refs):
     joined, (xq, own, other) = refs[:-3], refs[-3:]
     half = own.shape[1]
-    top, totals = 0, []
-    for part in joined:
-        wide = part.shape[1]
-        own[top : top + wide, :] = tn(part[...], xq[:, :half]).astype(BF)
-        other[top : top + wide, :] = tn(part[...], xq[:, half:]).astype(BF)
-        totals.append(jnp.sum(part[...].astype(F32), axis=0, keepdims=True))
-        top += wide
-    total = jnp.concatenate([*totals, jnp.zeros((1, 2 * half - top), F32)], axis=1)
-    below = own.shape[0] - top
+    wide = 3 * heads * HEAD
+    totals = [[], [], []]
+    for (start, number), part in zip(parts, joined):
+        span = number * HEAD
+        total = jnp.sum(part[...].astype(F32), axis=0, keepdims=True)
+        for out, lanes in ((own, slice(0, half)), (other, slice(half, 2 * half))):
+            grad = tn(part[...], xq[:, lanes]).astype(BF)
+            for i in range(3):
+                top = (i * heads + start) * HEAD
+                out[top : top + span, :] = grad[i * span : (i + 1) * span, :]
+        for i in range(3):
+            totals[i].append(total[:, i * span : (i + 1) * span])
+    total = jnp.concatenate([*totals[0], *totals[1], *totals[2], jnp.zeros((1, 2 * half - wide), F32)], axis=1)
+    below = own.shape[0] - wide
     sums = jnp.concatenate([total[:, :half], total[:, half:], jnp.zeros((below - 2, half), F32)], axis=0).astype(BF)
-    own[top:, :] = sums
-    other[top:, :] = sums
+    own[wide:, :] = sums
+    other[wide:, :] = sums
 
 
 def middle_kernel(plan, grid_rows, where, *refs):
@@ -797,7 +802,7 @@
     kv_got = after(to_col(kv_other), first_sum, second_sum)
     last_got, leaving, last_joined = join(dq, kv_own, kv_got)
     output = come_back(out_got)
-    in_own, in_other = call(project_in_grad_kernel, [((wide + 32, half), BF)] * 2, "vvv", us=6)(joined, last_joined, xq)
+    in_own, in_other = call(partial(project_in_grad_kernel, parts, heads), [((wide + 32, half), BF)] * 2, "vvv", us=6)(joined, last_joined, xq)
     in_got = to_col(in_other)
     last_got[0] = after(last_got[0], in_own)
     dx_own, dx_other = call(
@@ -810,13 +815,9 @@
     input_grad = come_back(dx_got)
     in_sum = reduce_groups(add(in_own, in_got), group, dx_pieces)
 
-    tops = [sum(spans[:i]) for i in range(6)]
-    in_parts = [in_sum[top : top + span] for top, span in zip(tops, spans)]
-    in_parts = [jnp.concatenate([in_parts[i], in_parts[3 + i]], axis=0) for i in range(3)]
-    project_in_grad = jnp.stack(in_parts).transpose(2, 0, 1)
+    project_in_grad = in_sum[:wide].reshape(3, inner, half).transpose(2, 0, 1)
     sums = in_sum[wide : wide + 2].reshape(2 * half)
-    in_sums = [sums[top : top + span] for top, span in zip(tops, spans)]
-    sums = [jnp.concatenate([in_sums[i], in_sums[3 + i]]) for i in (0, 2)]
+    sums = [sums[:inner], sums[2 * inner : 3 * inner]]
     tail = second_sum[plan["sums"]].astype(F32)
     return (
         output,

time: 387 us -> 389 us (level)
  Pallas kernels: 175 us -> 186 us
  starting transfers between devices: 92.4 us -> 85.5 us
    pallas_call x2, Pallas kernels: 57 us -> 64.5 us  [back(): call(partial(attend_back_kernel, grid_rows, heads, start, seqs, run, bloc...]
    ppermute x61, starting transfers between devices: 92.4 us -> 85.4 us  [shift(): lax.ppermute(array, axis, [(i, to(i)) for i in range(lax.axis_size(axis))])]
    pallas_call x1, Pallas kernels: 41.5 us -> 45.5 us  [local(): call(partial(attend_kernel, sizes, layout, heads, seqs, run), [((heads, h...]
  transfers between devices with their start and end apart: 63 -> 63, of which waited for: 17 -> 16; matrix products, arithmetic and copies ran while one was open for 7% -> 7% of each run, Pallas kernels for 37% -> 39%
where the time goes in v2:
time: 389 us; the launch traced here: 383 us
  Pallas kernels  186 us (48%)
  starting transfers between devices  85.5 us (22%)
  waiting for transfers between devices  59.9 us (15%)
  other arithmetic  19.1 us (5%)
  local copies, waits for them, and re-layouts  16.8 us (4%)
  between operations  15.2 us (4%)
    ppermute x61, starting transfers between devices, shift(): lax.ppermute(array, axis, [(i, to(i)) for i in range(lax.axis_size(axis))])  85.4 us
    pallas_call x2, Pallas kernels, back(): call(partial(attend_back_kernel, grid_rows, heads, start, seqs, run, bloc...  64.5 us
    ppermute x61, waiting for transfers between devices, shift(): lax.ppermute(array, axis, [(i, to(i)) for i in range(lax.axis_size(axis))])  59.8 us
    pallas_call x1, Pallas kernels, local(): call(partial(attend_kernel, sizes, layout, heads, seqs, run), [((heads, h...  45.5 us
    pallas_call x1, Pallas kernels, local(): call(partial(middle_kernel, plan, grid_rows), [((own_rows, half), BF), ((...  36.2 us
    unnamed x110, local copies, waits for them, and re-layouts  14.5 us
    convert_element_type x13, other arithmetic, add(): return sum((a.astype(F32) for a in arrays)).astype(BF)  12.8 us
  transfers between devices with their start and end apart: 63, of which 16 were waited for; matrix products, arithmetic and copies ran while one was open for 7% of the time, Pallas kernels for 39%

profile of v2, /device:TPU:0, one launch (start us, length us, event | category | flops | bytes accessed | tf_op | source)
XLA Modules:
  0.0 382.9 jit_solution(1273071692060983758)
XLA Ops:
  7.2 3.0 collective-permute-start.3
  12.3 2.8 shard_map.263
  25.2 6.7 %collective-permute-done.1 = bf16[256,384]{1,0:T(8,128)(2,1)S(1)} collective-permute-done((bf16[256,384]{1,0:T(8,128)(2,1)}, bf16[256,384]{1,0:T(8,128)(2,1)S(1)}, u32[]{:S(2)}, u32[]{:S(2)}) %collective-permute-start.1) | collective-permute-done | bytes 196640 | tf_op jit(solution)/shard_map/ppermute | solution.py:541
  35.3 4.7 %collective-permute-start.7 = (bf16[256,384]{1,0:T(8,128)(2,1)}, bf16[256,384]{1,0:T(8,128)(2,1)}, u32[]{:S(2)}, u32[]{:S(2)}) collective-permute-start(bf16[256,384]{1,0:T(8,128)(2,1)} %get-tuple-element.130), channel_id=1, source_target_pairs={{0,8},{8,16},{16,24},{24,0},{1,9},{9,17},{17,25},{25,1},{2,10},{10... | collective-permute-start | bytes 589832 | tf_op jit(solution)/shard_map/ppermute | solution.py:541
  48.1 5.3 %collective-permute-done.8.refs_2_ = bf16[256,384]{1,0:T(8,128)(2,1)} collective-permute-done((bf16[256,384]{1,0:T(8,128)(2,1)}, bf16[256,384]{1,0:T(8,128)(2,1)}, u32[]{:S(2)}, u32[]{:S(2)}) %collective-permute-start.8) | collective-permute-done | bytes 196640 | tf_op jit(solution)/shard_map/ppermute | solution.py:541
  57.8 7.5 %collective-permute-done.16.refs_6_ = bf16[512,384]{1,0:T(8,128)(2,1)S(1)} collective-permute-done((bf16[512,384]{1,0:T(8,128)(2,1)S(1)}, bf16[512,384]{1,0:T(8,128)(2,1)S(1)}, u32[]{:S(2)}, u32[]{:S(2)}) %collective-permute-start.16) | collective-permute-done | bytes 393248 | tf_op jit(solution)/shard_map/ppermute | solution.py:541
  72.9 45.5 %shard_map.266 = (bf16[3,2048,128]{2,1,0:T(8,128)(2,1)}, bf16[3,4096,128]{2,1,0:T(8,128)(2,1)}, bf16[3,4096,128]{2,1,0:T(8,128)(2,1)}, bf16[3,2048,64]{2,1,0:T(8...) custom-call(s32[128]{0:T(128)} %shard_map.264.place, ...), custom_call_target="tpu_custom_call" | custom-call | flops 14099999744 | bytes 47000000 | tf_op jit(solution)/shard_map/pallas_call | solution.py:677
  118.4 2.8 shard_map.267
  124.9 4.2 %collective-permute-done.22.refs_1_ = bf16[256,384]{1,0:T(8,128)(2,1)S(1)} collective-permute-done((bf16[256,384]{1,0:T(8,128)(2,1)S(1)}, bf16[256,384]{1,0:T(8,128)(2,1)S(1)}, u32[]{:S(2)}, u32[]{:S(2)}) %collective-permute-start.22) | collective-permute-done | bytes 196640 | tf_op jit(solution)/shard_map/ppermute | solution.py:541
  129.1 4.9 %collective-permute-done.23.refs_2_ = bf16[256,384]{1,0:T(8,128)(2,1)S(1)} collective-permute-done((bf16[256,384]{1,0:T(8,128)(2,1)S(1)}, bf16[256,384]{1,0:T(8,128)(2,1)S(1)}, u32[]{:S(2)}, u32[]{:S(2)}) %collective-permute-start.23) | collective-permute-done | bytes 196640 | tf_op jit(solution)/shard_map/ppermute | solution.py:541
  135.0 36.2 %shard_map.268 = (bf16[512,384]{1,0:T(8,128)(2,1)}, f32[512,768]{1,0:T(8,128)}, bf16[256,384]{1,0:T(8,128)(2,1)}, bf16[256,384]{1,0:T(8,128)(2,1)}, bf16[256,384...) custom-call(s32[3]{0:T(128)} %pad_add_fusion.where, ...), custom_call_target="tpu_custom_call" | custom-call | flops 12600000512 | bytes 42000000 | tf_op jit(solution)/shard_map/pallas_call | solution.py:721
  180.7 3.1 add_convert_fusion.1
  186.1 3.3 shard_map.269
  191.3 6.3 %collective-permute-start.34 = (bf16[256,384]{1,0:T(8,128)(2,1)}, bf16[256,384]{1,0:T(8,128)(2,1)S(1)}, u32[]{:S(2)}, u32[]{:S(2)}) collective-permute-start(bf16[256,384]{1,0:T(8,128)(2,1)} %get-tuple-element.177), channel_id=1, source_target_pairs={{0,8},{8,16},{16,24},{24,0},{1,9},{9,17},{17,25},{25,1},{2,10},{10... | collective-permute-start | bytes 589832 | tf_op jit(solution)/shard_map/ppermute | solution.py:541
  197.6 4.3 %collective-permute-start.35 = (bf16[256,384]{1,0:T(8,128)(2,1)}, bf16[256,384]{1,0:T(8,128)(2,1)S(1)}, u32[]{:S(2)}, u32[]{:S(2)}) collective-permute-start(bf16[256,384]{1,0:T(8,128)(2,1)} %get-tuple-element.178), channel_id=1, source_target_pairs={{0,16},{8,24},{16,0},{24,8},{1,17},{9,25},{17,1},{25,9},{2,18},{10... | collective-permute-start | bytes 589832 | tf_op jit(solution)/shard_map/ppermute | solution.py:541
  201.9 40.2 %shard_map.270 = (bf16[2,2048,64]{2,1,0:T(8,128)(2,1)}, f32[2,2048,128]{2,1,0:T(8,128)}, bf16[2,2048,128]{2,1,0:T(8,128)(2,1)}) custom-call(s32[3]{0:T(128)} %pad_add_fusion.where, s32[1,4]{1,0:T(1,128)} %lengths.5, bf16[3,2048,128]{2,1,0:T(8,128)(2,1)} %get-tuple-element.171.q_ref, bf16[3,4096,128]{2,1,0:T(8,128)(2,1)} %get-tuple-element.172.k_ref, ...), custom_call_target="tpu_custom_call" | custom-call | flops 9600000000 | bytes 32000000 | tf_op jit(solution)/shard_map/pallas_call | solution.py:760
  248.7 4.3 %shard_map.271 = (bf16[256,768]{1,0:T(8,128)(2,1)}, bf16[256,768]{1,0:T(8,128)(2,1)}, bf16[256,768]{1,0:T(8,128)(2,1)}, bf16[256,768]{1,0:T(8,128)(2,1)}, bf16[2048,384]{1,0:T(8,128)(2,1)}) custom-call(s32[3]{0:T(128)} %pad_add_fusion.where, bf16[2,2048,64]{2,1,0:T(8,128)(2,1)} %get-tuple-element.181.dq_ref, f32[2,2048,128]{2,1,0:T(8,128)} %get-tuple-element.185.own_ref, ...), custom_call_target="tpu_custom_call" | custom-call | flops 1200000000 | bytes 4000000 | tf_op jit(solution)/shard_map/pallas_call | solution.py:780
  256.5 24.3 %shard_map.272 = (bf16[1,2048,64]{2,1,0:T(8,128)(2,1)}, f32[1,2048,128]{2,1,0:T(8,128)}, bf16[1,2048,128]{2,1,0:T(8,128)(2,1)}) custom-call(s32[3]{0:T(128)} %pad_add_fusion.where, s32[1,4]{1,0:T(1,128)} %lengths.5, bf16[3,2048,128]{2,1,0:T(8,128)(2,1)} %get-tuple-element.171.q_ref, bf16[3,4096,128]{2,1,0:T(8,128)(2,1)} %get-tuple-element.172.k_ref, ...), custom_call_target="tpu_custom_call" | custom-call | flops 4800000000 | bytes 16000000 | tf_op jit(solution)/shard_map/pallas_call | solution.py:760
  290.0 3.0 shard_map.274
  293.0 6.2 %shard_map.275 = (bf16[608,384]{1,0:T(8,128)(2,1)}, bf16[608,384]{1,0:T(8,128)(2,1)}) custom-call(bf16[2048,384]{1,0:T(8,128)(2,1)} %get-tuple-element.202.refs_0_, bf16[2048,192]{1,0:T(8,128)(2,1)} %get-tuple-element.203.refs_1_, bf16[2048,768]{1,0:T(8,128)(2,1)} %get-tuple-element.204.refs_2_), custom_call_target="tpu_custom_call" | custom-call | flops 1800000000 | bytes 6000000 | tf_op jit(solution)/shard_map/pallas_call | solution.py:805
  311.6 7.1 %shard_map.276 = (bf16[512,384]{1,0:T(8,128)(2,1)}, bf16[512,384]{1,0:T(8,128)(2,1)}) custom-call(s32[3]{0:T(128)} %pad_add_fusion.where, bf16[256,768]{1,0:T(8,128)(2,1)} %get-tuple-element.188.refs_0_, bf16[256,768]{1,0:T(8,128)(2,1)} %collective-permute-done.38.refs_1_, bf16[256,768]{1,0:T(8,128)(2,1)} %collective-permute-done.39.refs_2_, ...), custom_call_target="tpu_custom_call" | custom-call | flops 2100000000 | bytes 7000000 | tf_op jit(solution)/shard_map/pallas_call | solution.py:808
  329.2 16.2 %collective-permute-start.57 = (bf16[496,384]{1,0:T(8,128)(2,1)S(1)}, bf16[496,384]{1,0:T(8,128)(2,1)S(1)}, u32[]{:S(2)}, u32[]{:S(2)}) collective-permute-start(bf16[496,384]{1,0:T(8,128)(2,1)S(1)} %add_convert_fusion.6), channel_id=1, source_target_pairs={{0,8},{8,0},{16,24},{24,16},{1,9},{9,1},{17,25},{25,17},{2,10},{10... | collective-permute-start | bytes 1142792 | tf_op jit(solution)/shard_map/ppermute | solution.py:541
  352.6 14.0 %collective-permute-done.60 = bf16[192,768]{1,0:T(8,128)(2,1)S(1)} collective-permute-done((bf16[192,768]{1,0:T(8,128)(2,1)S(1)}, bf16[192,768]{1,0:T(8,128)(2,1)S(1)}, u32[]{:S(2)}, u32[]{:S(2)}) %collective-permute-start.60) | collective-permute-done | bytes 294944 | tf_op jit(solution)/shard_map/ppermute | solution.py:541
  371.0 2.9 collective-permute-done.54
  (273 shorter events, 109.1 us)
Async XLA Ops:
  7.2 126.8 %all-gather.5.cloned.1.call-start = ((), (), s32[]{:S(2)}) async-start(), calls=%async_computation | async-start | bytes 6746112 | tf_op jit(solution)/shard_map/all_gather | solution.py:671
  7.2 24.7 %collective-permute-start.3 = (bf16[384,768]{1,0:T(8,128)(2,1)}, bf16[384,768]{1,0:T(8,128)(2,1)}, u32[]{:S(2)}, u32[]{:S(2)}) collective-permute-start(bf16[384,768]{1,0:T(8,128)(2,1)} %refs_7_), channel_id=1, source_target_pairs={{0,2},{2,0},{4,6},{6,4},{1,3},{3,1},{5,7},{7,5},{8,10},{10,8},{12,... | collective-permute-start | bytes 1769480 | tf_op jit(solution)/shard_map/ppermute | solution.py:541
  10.2 21.7 %collective-permute-start.4 = (bf16[384,768]{1,0:T(8,128)(2,1)}, bf16[384,768]{1,0:T(8,128)(2,1)}, u32[]{:S(2)}, u32[]{:S(2)}) collective-permute-start(bf16[384,768]{1,0:T(8,128)(2,1)} %refs_7_), channel_id=1, source_target_pairs={{0,4},{2,6},{4,0},{6,2},{1,5},{3,7},{5,1},{7,3},{8,12},{10,14},{12... | collective-permute-start | bytes 1769480 | tf_op jit(solution)/shard_map/ppermute | solution.py:541
  32.1 21.3 %collective-permute-start.5 = (bf16[1024,384]{1,0:T(8,128)(2,1)S(1)}, bf16[1024,384]{1,0:T(8,128)(2,1)S(1)}, u32[]{:S(2)}, u32[]{:S(2)}) collective-permute-start(bf16[1024,384]{1,0:T(8,128)(2,1)S(1)} %constant_dynamic-update-slice_fusion.refs_0_), channel_id=1, source_target_pairs={{0,2},{2,0},{4,6},{6,4},{1,3},{3,1},{5,7},{7,5},{8,10},{10,8},{12,... | collective-permute-start | bytes 2359304 | tf_op jit(solution)/shard_map/ppermute | solution.py:541
  53.4 255.7 %all-gather.7.cloned.1.call-start = ((), (), s32[]{:S(2)}) async-start(), calls=%async_computation.1 | async-start | bytes 3981312 | tf_op jit(solution)/shard_map/all_gather | solution.py:718
  67.7 50.7 %collective-permute-start.21 = (bf16[384,768]{1,0:T(8,128)(2,1)}, bf16[384,768]{1,0:T(8,128)(2,1)S(1)}, u32[]{:S(2)}, u32[]{:S(2)}) collective-permute-start(bf16[384,768]{1,0:T(8,128)(2,1)} %refs_7_), channel_id=1, source_target_pairs={{0,6},{2,4},{4,2},{6,0},{1,7},{3,5},{5,3},{7,1},{8,14},{10,12},{12... | collective-permute-start | bytes 1769480 | tf_op jit(solution)/shard_map/ppermute | solution.py:541
  189.4 53.3 %collective-permute-start.33 = (bf16[1984,384]{1,0:T(8,128)(2,1)}, bf16[1984,384]{1,0:T(8,128)(2,1)}, u32[]{:S(2)}, u32[]{:S(2)}) collective-permute-start(bf16[1984,384]{1,0:T(8,128)(2,1)} %add_convert_fusion), channel_id=1, source_target_pairs={{0,4},{2,6},{4,0},{6,2},{1,5},{3,7},{5,1},{7,3},{8,12},{10,14},{12... | collective-permute-start | bytes 4571144 | tf_op jit(solution)/shard_map/ppermute | solution.py:541
  190.8 51.3 %collective-permute-start.32 = (bf16[2,384,768]{2,1,0:T(8,128)(2,1)S(1)}, bf16[2,384,768]{2,1,0:T(8,128)(2,1)}, u32[]{:S(2)}, u32[]{:S(2)}) collective-permute-start(bf16[2,384,768]{2,1,0:T(8,128)(2,1)S(1)} %copy-done.3), channel_id=1, source_target_pairs={{0,2},{2,0},{4,6},{6,4},{1,3},{3,1},{5,7},{7,5},{8,10},{10,8},{12,... | collective-permute-start | bytes 3538952 | tf_op jit(solution)/shard_map/ppermute | solution.py:541
  191.3 50.8 %collective-permute-start.34 = (bf16[256,384]{1,0:T(8,128)(2,1)}, bf16[256,384]{1,0:T(8,128)(2,1)S(1)}, u32[]{:S(2)}, u32[]{:S(2)}) collective-permute-start(bf16[256,384]{1,0:T(8,128)(2,1)} %get-tuple-element.177), channel_id=1, source_target_pairs={{0,8},{8,16},{16,24},{24,0},{1,9},{9,17},{17,25},{25,1},{2,10},{10... | collective-permute-start | bytes 589832 | tf_op jit(solution)/shard_map/ppermute | solution.py:541
  197.6 44.5 %collective-permute-start.35 = (bf16[256,384]{1,0:T(8,128)(2,1)}, bf16[256,384]{1,0:T(8,128)(2,1)S(1)}, u32[]{:S(2)}, u32[]{:S(2)}) collective-permute-start(bf16[256,384]{1,0:T(8,128)(2,1)} %get-tuple-element.178), channel_id=1, source_target_pairs={{0,16},{8,24},{16,0},{24,8},{1,17},{9,25},{17,1},{25,9},{2,18},{10... | collective-permute-start | bytes 589832 | tf_op jit(solution)/shard_map/ppermute | solution.py:541
  201.9 40.2 %collective-permute-start.36 = (bf16[256,384]{1,0:T(8,128)(2,1)}, bf16[256,384]{1,0:T(8,128)(2,1)}, u32[]{:S(2)}, u32[]{:S(2)}) collective-permute-start(bf16[256,384]{1,0:T(8,128)(2,1)} %get-tuple-element.179), channel_id=1, source_target_pairs={{0,24},{8,0},{16,8},{24,16},{1,25},{9,1},{17,9},{25,17},{2,26},{10... | collective-permute-start | bytes 589832 | tf_op jit(solution)/shard_map/ppermute | solution.py:541
  244.3 36.5 %collective-permute-start.41 = (bf16[384,768]{1,0:T(8,128)(2,1)S(1)}, bf16[384,768]{1,0:T(8,128)(2,1)}, u32[]{:S(2)}, u32[]{:S(2)}) collective-permute-start(bf16[384,768]{1,0:T(8,128)(2,1)S(1)} %fusion.3), channel_id=1, source_target_pairs={{0,4},{2,6},{4,0},{6,2},{1,5},{3,7},{5,1},{7,3},{8,12},{10,14},{12... | collective-permute-start | bytes 1769480 | tf_op jit(solution)/shard_map/ppermute | solution.py:541
  247.2 35.4 %collective-permute-start.42 = (bf16[992,384]{1,0:T(8,128)(2,1)S(1)}, bf16[992,384]{1,0:T(8,128)(2,1)}, u32[]{:S(2)}, u32[]{:S(2)}) collective-permute-start(bf16[992,384]{1,0:T(8,128)(2,1)S(1)} %add_convert_fusion.3), channel_id=1, source_target_pairs={{0,2},{2,0},{4,6},{6,4},{1,3},{3,1},{5,7},{7,5},{8,10},{10,8},{12,... | collective-permute-start | bytes 2285576 | tf_op jit(solution)/shard_map/ppermute | solution.py:541
  253.0 29.6 %collective-permute-start.38 = (bf16[256,768]{1,0:T(8,128)(2,1)}, bf16[256,768]{1,0:T(8,128)(2,1)}, u32[]{:S(2)}, u32[]{:S(2)}) collective-permute-start(bf16[256,768]{1,0:T(8,128)(2,1)} %get-tuple-element.189), channel_id=1, source_target_pairs={{0,2},{2,0},{4,6},{6,4},{1,3},{3,1},{5,7},{7,5},{8,10},{10,8},{12,... | collective-permute-start | bytes 1179656 | tf_op jit(solution)/shard_map/ppermute | solution.py:541
  253.5 29.1 %collective-permute-start.39 = (bf16[256,768]{1,0:T(8,128)(2,1)}, bf16[256,768]{1,0:T(8,128)(2,1)}, u32[]{:S(2)}, u32[]{:S(2)}) collective-permute-start(bf16[256,768]{1,0:T(8,128)(2,1)} %get-tuple-element.190), channel_id=1, source_target_pairs={{0,4},{2,6},{4,0},{6,2},{1,5},{3,7},{5,1},{7,3},{8,12},{10,14},{12... | collective-permute-start | bytes 1179656 | tf_op jit(solution)/shard_map/ppermute | solution.py:541
  254.6 29.2 %collective-permute-start.40 = (bf16[256,768]{1,0:T(8,128)(2,1)}, bf16[256,768]{1,0:T(8,128)(2,1)}, u32[]{:S(2)}, u32[]{:S(2)}) collective-permute-start(bf16[256,768]{1,0:T(8,128)(2,1)} %get-tuple-element.191), channel_id=1, source_target_pairs={{0,6},{2,4},{4,2},{6,0},{1,7},{3,5},{5,3},{7,1},{8,14},{10,12},{12... | collective-permute-start | bytes 1179656 | tf_op jit(solution)/shard_map/ppermute | solution.py:541
  303.3 23.3 %collective-permute-start.56 = (bf16[496,384]{1,0:T(8,128)(2,1)S(1)}, bf16[496,384]{1,0:T(8,128)(2,1)S(1)}, u32[]{:S(2)}, u32[]{:S(2)}) collective-permute-start(bf16[496,384]{1,0:T(8,128)(2,1)S(1)} %add_convert_fusion.7), channel_id=1, source_target_pairs={{0,24},{8,16},{16,8},{24,0},{1,25},{9,17},{17,9},{25,1},{2,26},{10... | collective-permute-start | bytes 1142792 | tf_op jit(solution)/shard_map/ppermute | solution.py:541
  307.4 21.8 %collective-permute-start.59 = (bf16[192,768]{1,0:T(8,128)(2,1)S(1)}, bf16[192,768]{1,0:T(8,128)(2,1)S(1)}, u32[]{:S(2)}, u32[]{:S(2)}) collective-permute-start(bf16[192,768]{1,0:T(8,128)(2,1)S(1)} %add_convert_fusion.9), channel_id=1, source_target_pairs={{0,24},{8,16},{16,8},{24,0},{1,25},{9,17},{17,9},{25,1},{2,26},{10... | collective-permute-start | bytes 884744 | tf_op jit(solution)/shard_map/ppermute | solution.py:541
  318.9 26.5 %collective-permute-start.52 = (bf16[304,384]{1,0:T(8,128)(2,1)S(1)}, bf16[304,384]{1,0:T(8,128)(2,1)S(1)}, u32[]{:S(2)}, u32[]{:S(2)}) collective-permute-start(bf16[304,384]{1,0:T(8,128)(2,1)S(1)} %broadcast_select_fusion.8), channel_id=1, source_target_pairs={{0,8},{8,0},{16,24},{24,16},{1,9},{9,1},{17,25},{25,17},{2,10},{10... | collective-permute-start | bytes 700424 | tf_op jit(solution)/shard_map/ppermute | solution.py:541
  324.4 21.2 %collective-permute-start.48 = (bf16[256,384]{1,0:T(8,128)(2,1)}, bf16[256,384]{1,0:T(8,128)(2,1)S(1)}, u32[]{:S(2)}, u32[]{:S(2)}) collective-permute-start(bf16[256,384]{1,0:T(8,128)(2,1)} %get-tuple-element.215), channel_id=1, source_target_pairs={{0,8},{8,16},{16,24},{24,0},{1,9},{9,17},{17,25},{25,1},{2,10},{10... | collective-permute-start | bytes 589832 | tf_op jit(solution)/shard_map/ppermute | solution.py:541
  326.1 22.9 %collective-permute-start.49 = (bf16[256,384]{1,0:T(8,128)(2,1)}, bf16[256,384]{1,0:T(8,128)(2,1)S(1)}, u32[]{:S(2)}, u32[]{:S(2)}) collective-permute-start(bf16[256,384]{1,0:T(8,128)(2,1)} %get-tuple-element.216), channel_id=1, source_target_pairs={{0,16},{8,24},{16,0},{24,8},{1,17},{9,25},{17,1},{25,9},{2,18},{10... | collective-permute-start | bytes 589832 | tf_op jit(solution)/shard_map/ppermute | solution.py:541
  326.6 22.4 %collective-permute-start.50 = (bf16[256,384]{1,0:T(8,128)(2,1)}, bf16[256,384]{1,0:T(8,128)(2,1)S(1)}, u32[]{:S(2)}, u32[]{:S(2)}) collective-permute-start(bf16[256,384]{1,0:T(8,128)(2,1)} %get-tuple-element.217), channel_id=1, source_target_pairs={{0,24},{8,0},{16,8},{24,16},{1,25},{9,1},{17,9},{25,17},{2,26},{10... | collective-permute-start | bytes 589832 | tf_op jit(solution)/shard_map/ppermute | solution.py:541
  329.2 38.7 %collective-permute-start.57 = (bf16[496,384]{1,0:T(8,128)(2,1)S(1)}, bf16[496,384]{1,0:T(8,128)(2,1)S(1)}, u32[]{:S(2)}, u32[]{:S(2)}) collective-permute-start(bf16[496,384]{1,0:T(8,128)(2,1)S(1)} %add_convert_fusion.6), channel_id=1, source_target_pairs={{0,8},{8,0},{16,24},{24,16},{1,9},{9,1},{17,25},{25,17},{2,10},{10... | collective-permute-start | bytes 1142792 | tf_op jit(solution)/shard_map/ppermute | solution.py:541
  345.6 22.1 %collective-permute-start.53 = (bf16[304,384]{1,0:T(8,128)(2,1)S(1)}, bf16[304,384]{1,0:T(8,128)(2,1)S(1)}, u32[]{:S(2)}, u32[]{:S(2)}) collective-permute-start(bf16[304,384]{1,0:T(8,128)(2,1)S(1)} %add_convert_fusion.11), channel_id=1, source_target_pairs={{0,24},{8,16},{16,8},{24,0},{1,25},{9,17},{17,9},{25,1},{2,26},{10... | collective-permute-start | bytes 700424 | tf_op jit(solution)/shard_map/ppermute | solution.py:541
  (87 other events, 800.6 us)
Sparse Core Ops, SparseCore 0:
  53.6 60.0 all-gather.4
  175.8 53.0 all-gather.6
